TPU v7x, 128 devices: a whole 4x4x4 slice. The times are simulated.
128 devices in a mesh: row: 16 (over z, y_lo, core), col: 8 (over x, y_hi).
Axes of the slice: x: 4, y: 4 (y_hi: 2, y_lo: 2; y = y_hi * 2 + y_lo), z: 4, core: 2. Of those that a mesh axis runs over, the one named last changes fastest.
Arguments:
- image: bfloat16 [128, 1024, 768], P('row', 'col'), may hold values from -6 to 6
- skip_rows: bfloat16 [131072, 768], P(('row', 'col')), may hold values from -6 to 6
- owners: int32 [131072, 1], P(('row', 'col')), may hold values from 0 to 127, as said below
- positions: int32 [131072], P(('row', 'col')), may hold values from 0 to 1023, as said below
- gain: float32 [768], replicated, may hold values from 0.5 to 1.5
- w_qkv: bfloat16 [768, 2304], replicated, may hold values from -0.21875 to 0.21875
- w_out: bfloat16 [768, 768], replicated, may hold values from -0.4375 to 0.4375
- head_scale: float32 [12], replicated, may hold values from 4 to 300
Outputs:
- level_out: bfloat16 [128, 1024, 768], P('row', 'col')
Inputs may be any that keep to these rules, and one draw needn't show every extreme that they name: `owners`: at most 16 of the 1024 rows of one device name one owner, and some device sends exactly 16 rows to some owner; every owner is named by exactly 1024 rows in all. The pairs (owners, positions) name every cell of the image exactly once.
All inputs are finite; a program needn't handle non-finite values.
Results may differ from a plain program's by a relative error of at most 0.017.
The roundings to bfloat16 on the way count: a program that leaves them out, or rounds other values in their place, can miss the bound.
Values may be sent and summed in bfloat16 or wider, within the bound.
A program may use at most 128 MiB of HBM per device.

v0:
```python
import functools

import jax
import jax.numpy as jnp
from jax import lax
from jax.experimental import pallas as pl
from jax.experimental.pallas import tpu as pltpu
from jax.sharding import PartitionSpec as P

RIM = 3
PAD = 8
GROUP_ROWS = 4
GROUP_COLS = 16
HEAD = 64
QUAD = 256


def dot(a, b):
    return jnp.dot(a, b, preferred_element_type=jnp.float32)


def dot_nt(a, b):
    return lax.dot_general(a, b, (((1,), (1,)), ((), ())), preferred_element_type=jnp.float32)


def head_sums(x, ones):
    square = x * x
    high = square.astype(jnp.bfloat16)
    low = (square - high.astype(jnp.float32)).astype(jnp.bfloat16)
    width = x.shape[1]
    parts = []
    for start in range(0, width, QUAD):
        lanes = slice(start, start + QUAD)
        parts.append(dot(high[:, lanes], ones) + dot(low[:, lanes], ones))
    return jnp.concatenate(parts, axis=1)


def attend_kernel(
    normed_ref, skip_ref, image_ref, w_qkv_ref, w_out_ref, scale_ref, out_ref,
    query_s, key_s, value_s, attended_s,
):
    ext_rows, ext_cols, width = normed_ref.shape
    tile_rows, tile_cols, _ = image_ref.shape
    image_rows = tile_rows * lax.axis_size("row")
    image_cols = tile_cols * lax.axis_size("col")
    row_base = lax.axis_index("row") * tile_rows
    col_base = lax.axis_index("col") * tile_cols
    lane_a = lax.broadcasted_iota(jnp.int32, (QUAD, QUAD), 0) // HEAD
    lane_b = lax.broadcasted_iota(jnp.int32, (QUAD, QUAD), 1) // HEAD
    ones = (lane_a == lane_b).astype(jnp.float32).astype(jnp.bfloat16)

    def keyval_step(step, carry):
        x = normed_ref[pl.ds(step * 2, 2)].reshape(2 * ext_cols, width)
        keys = dot(x, w_qkv_ref[:, width : 2 * width]).astype(jnp.bfloat16)
        keys = keys.astype(jnp.float32)
        unit = keys * lax.rsqrt(head_sums(keys, ones) + 1e-06)
        key_s[pl.ds(step * 2, 2)] = unit.astype(jnp.bfloat16).reshape(2, ext_cols, width)
        values = dot(x, w_qkv_ref[:, 2 * width :])
        value_s[pl.ds(step * 2, 2)] = values.astype(jnp.bfloat16).reshape(2, ext_cols, width)
        return carry

    lax.fori_loop(0, ext_rows // 2, keyval_step, 0)

    def query_step(step, carry):
        x = normed_ref[pl.ds(step * 2 + RIM, 2), PAD : PAD + tile_cols]
        queries = dot(x.reshape(2 * tile_cols, width), w_qkv_ref[:, :width])
        unit = queries * scale_ref[...] * lax.rsqrt(head_sums(queries, ones) + 1e-06)
        query_s[pl.ds(step * 2, 2)] = unit.astype(jnp.bfloat16).reshape(2, tile_cols, width)
        return carry

    lax.fori_loop(0, tile_rows // 2, query_step, 0)

    key_rows = GROUP_ROWS + 2 * RIM
    key_cols = GROUP_COLS + 2 * PAD
    n_query = GROUP_ROWS * GROUP_COLS
    n_key = key_rows * key_cols
    col_groups = tile_cols // GROUP_COLS
    query_at = lax.broadcasted_iota(jnp.int32, (n_query, n_key), 0)
    key_at = lax.broadcasted_iota(jnp.int32, (n_query, n_key), 1)
    row_gap = key_at // key_cols - query_at // GROUP_COLS
    col_gap = key_at % key_cols - query_at % GROUP_COLS
    near = (
        (row_gap >= 0)
        & (row_gap <= 2 * RIM)
        & (col_gap >= PAD - RIM)
        & (col_gap <= PAD + RIM)
    )
    lane_head = lax.broadcasted_iota(jnp.int32, (1, QUAD), 1) // HEAD
    heads = QUAD // HEAD

    def attend_step(step, carry):
        row_at = (step // col_groups) * GROUP_ROWS
        col_at = pl.multiple_of((step % col_groups) * GROUP_COLS, GROUP_COLS)
        key_row = row_base + row_at - RIM + key_at // key_cols
        key_col = col_base + col_at - PAD + key_at % key_cols
        inside = (
            near & (key_row >= 0) & (key_row < image_rows) & (key_col >= 0) & (key_col < image_cols)
        )
        bias = jnp.where(inside, 0.0, -1e30)
        for start in range(0, width, QUAD):
            lanes = slice(start, start + QUAD)
            query = query_s[pl.ds(row_at, GROUP_ROWS), pl.ds(col_at, GROUP_COLS), lanes]
            query = query.reshape(n_query, QUAD)
            keys = key_s[pl.ds(row_at, key_rows), pl.ds(col_at, key_cols), lanes]
            keys = keys.reshape(n_key, QUAD)
            values = value_s[pl.ds(row_at, key_rows), pl.ds(col_at, key_cols), lanes]
            values = values.reshape(n_key, QUAD)
            spread = jnp.concatenate(
                [
                    query * (lane_head == h).astype(jnp.float32).astype(jnp.bfloat16)
                    for h in range(heads)
                ],
                axis=0,
            )
            scores = dot_nt(spread, keys)
            scores = (scores.reshape(heads, n_query, n_key) + bias[None]).reshape(-1, n_key)
            top = jnp.max(scores, axis=1, keepdims=True)
            expo = jnp.exp(scores - top)
            inverse = 1.0 / jnp.sum(expo, axis=1, keepdims=True)
            mixed = dot((expo * inverse).astype(jnp.bfloat16), values)
            joined = mixed[:n_query]
            for h in range(1, heads):
                part = mixed[h * n_query : (h + 1) * n_query]
                joined = jnp.where(lane_head == h, part, joined)
            attended_s[pl.ds(row_at, GROUP_ROWS), pl.ds(col_at, GROUP_COLS), lanes] = (
                joined.astype(jnp.bfloat16).reshape(GROUP_ROWS, GROUP_COLS, QUAD)
            )
        return carry

    lax.fori_loop(0, (tile_rows // GROUP_ROWS) * col_groups, attend_step, 0)

    def out_step(step, carry):
        rows = pl.ds(step * 2, 2)
        resid = image_ref[rows].astype(jnp.float32) + skip_ref[rows].astype(jnp.float32)
        projected = dot(attended_s[rows].reshape(2 * tile_cols, width), w_out_ref[...])
        out_ref[rows] = (resid + projected.reshape(2, tile_cols, width)).astype(jnp.bfloat16)
        return carry

    lax.fori_loop(0, tile_rows // 2, out_step, 0)


def attend(normed, skip, image, w_qkv, w_out, scale):
    tile_rows, tile_cols, width = image.shape
    vmem = pl.BlockSpec(memory_space=pltpu.VMEM)
    return pl.pallas_call(
        attend_kernel,
        out_shape=jax.ShapeDtypeStruct(image.shape, jnp.bfloat16),
        in_specs=[vmem] * 6,
        out_specs=vmem,
        scratch_shapes=[
            pltpu.VMEM(image.shape, jnp.bfloat16),
            pltpu.VMEM(normed.shape, jnp.bfloat16),
            pltpu.VMEM(normed.shape, jnp.bfloat16),
            pltpu.VMEM(image.shape, jnp.bfloat16),
        ],
        compiler_params=pltpu.CompilerParams(vmem_limit_bytes=56 << 20),
        name="attend",
    )(normed, skip, image, w_qkv, w_out, scale)


def extended(array, axis, dim, width, pad):
    peers, length = (lax.axis_size(axis), array.shape[dim])
    up = [(i, i + 1) for i in range(peers - 1)]
    down = [(j, i) for i, j in up]
    last = lax.slice_in_dim(array, length - width, length, axis=dim)
    first = lax.slice_in_dim(array, 0, width, axis=dim)
    before = lax.ppermute(last, axis, up)
    after = lax.ppermute(first, axis, down)
    blank = list(array.shape)
    blank[dim] = pad - width
    blank = jnp.zeros(blank, array.dtype)
    return jnp.concatenate([blank, before, array, after, blank], axis=dim)


def local(image, skip_rows, owners, positions, gain, w_qkv, w_out, head_scale):
    tile_rows, tile_cols, model_width = image.shape
    device_count = lax.axis_size("row") * lax.axis_size("col")
    rows_held = skip_rows.shape[0]
    capacity = 2 * rows_held // device_count
    cell_count = tile_rows * tile_cols
    owner_ids = owners[:, 0]
    one_hot = (owner_ids[:, None] == jnp.arange(device_count, dtype=jnp.int32)[None, :]).astype(
        jnp.int32
    )
    earlier = jnp.cumsum(one_hot, axis=0) - one_hot
    row_rank = jnp.sum(earlier * one_hot, axis=1)
    slot_index = owner_ids * capacity + row_rank
    send_rows = (
        jnp.zeros((device_count * capacity, model_width), jnp.bfloat16)
        .at[slot_index]
        .set(skip_rows)
    )
    send_cells = (
        jnp.full((device_count * capacity,), cell_count, jnp.int32).at[slot_index].set(positions)
    )
    got_rows, got_cells = (
        lax.all_to_all(
            send_rows.reshape(device_count, capacity, model_width),
            ("row", "col"),
            split_axis=0,
            concat_axis=0,
            tiled=True,
        ),
        lax.all_to_all(
            send_cells.reshape(device_count, capacity),
            ("row", "col"),
            split_axis=0,
            concat_axis=0,
            tiled=True,
        ),
    )
    skip = jnp.zeros((cell_count, model_width), jnp.bfloat16)
    skip = skip.at[got_cells.reshape(-1)].set(got_rows.reshape(-1, model_width), mode="drop")
    skip = skip.reshape(tile_rows, tile_cols, model_width)
    resid = image.astype(jnp.float32) + skip.astype(jnp.float32)
    normed = (
        resid * lax.rsqrt(jnp.mean(resid * resid, axis=-1, keepdims=True) + 1e-06) * gain
    ).astype(jnp.bfloat16)
    normed = extended(normed, "row", 0, RIM, RIM)
    normed = extended(normed, "col", 1, RIM, PAD)
    scale = jnp.repeat(head_scale, HEAD)[None, :]
    return attend(normed, skip, image, w_qkv, w_out, scale)


def solution(mesh):
    in_specs = (
        P("row", "col", None),
        P(("row", "col"), None),
        P(("row", "col"), None),
        P(("row", "col")),
        P(),
        P(),
        P(),
        P(),
    )
    out_specs = P("row", "col", None)
    return jax.shard_map(local, mesh=mesh, in_specs=in_specs, out_specs=out_specs, check_vma=False)
```

profile of v0, /device:TPU:11, one launch (start us, length us, event | category | flops | bytes accessed | tf_op | source)
XLA Modules:
  0.0 159.3 jit_solution(9049137614190747749)
XLA Ops:
  0.0 0.0 copy-start.2
  0.0 0.9 copy.12
  0.9 0.2 fusion.6
  1.2 0.1 copy.13
  1.3 0.0 copy-done.2
  1.3 0.4 fusion.5
  1.7 4.5 %scatter_custom_fusion = s32[2048]{0:T(1024)S(1)} fusion(s32[1024]{0:T(1024)S(1)} %bitcast.27, s32[1024]{0:T(1024)} %param.11, s32[]{:T(128)} %constant.9.clone.1), kind=kCustom, calls=%fused_computation.24 | custom fusion | bytes 8704 | tf_op jit(solution)/shard_map/scatter | solution.py:194
  6.1 0.7 all_to_all.9
  6.9 10.7 %all-to-all-start = ((s32[128,1,16]{2,1,0:T(1,128)}), s32[128,1,16]{2,1,0:T(1,128)S(1)}, u32[]{:S(2)}, u32[]{:S(2)}) async-start(s32[128,1,16]{2,1,0:T(1,128)} %bitcast.7), calls=%async_computation | async-start | bytes 131072 | tf_op jit(solution)/shard_map/all_to_all | solution.py:204
  17.6 7.9 %scatter_custom_fusion.1 = bf16[2048,768]{1,0:T(8,128)(2,1)} fusion(s32[1024]{0:T(1024)S(1)} %bitcast.28, bf16[1024,768]{1,0:T(8,128)(2,1)} %param.9, bf16[]{:T(256)} %constant.8.clone.1), kind=kCustom, calls=%fused_computation.7 | custom fusion | bytes 3146240 | tf_op jit(solution)/shard_map/scatter | solution.py:191
  25.5 0.0 all-to-all-done
  25.5 0.0 copy-start.1
  25.5 10.2 %all-to-all-start.1 = ((bf16[128,16,768]{2,1,0:T(8,128)(2,1)}), bf16[128,16,768]{2,1,0:T(8,128)(2,1)}, u32[]{:S(2)}, u32[]{:S(2)}) async-start(bf16[128,16,768]{2,1,0:T(8,128)(2,1)} %bitcast.22), calls=%async_computation.1 | async-start | bytes 6291456 | tf_op jit(solution)/shard_map/all_to_all | solution.py:197
  35.7 0.0 copy-start.3
  35.7 0.5 broadcast.70
  36.2 0.8 reduce.3
  37.1 0.1 reshape.72
  37.2 37.5 %all-to-all-done.1 = bf16[128,16,768]{2,1,0:T(8,128)(2,1)} async-done(((bf16[128,16,768]{2,1,0:T(8,128)(2,1)}), bf16[128,16,768]{2,1,0:T(8,128)(2,1)}, u32[]{:S(2)}, u32[]{:S(2)}) %all-to-all-start.1) | async-done | bytes 3145760 | tf_op jit(solution)/shard_map/all_to_all | solution.py:197
  74.6 10.6 %scatter_custom_fusion.2 = bf16[1024,768]{1,0:T(8,128)(2,1)S(1)} fusion(s32[2048]{0:T(1024)S(1)} %bitcast.26, bf16[2048,768]{1,0:T(8,128)(2,1)} %bitcast.10, bf16[]{:T(256)} %constant.8.clone.1), kind=kCustom, calls=%fused_computation.9 | custom fusion | bytes 1573376 | tf_op jit(solution)/shard_map/scatter | solution.py:213
  85.2 0.0 copy-start
  85.3 0.0 copy-done.1
  85.3 0.6 multiply_reduce_fusion
  85.9 0.0 copy-done.3
  85.9 0.6 multiply_convert_fusion
  86.4 0.0 copy-done
  86.5 0.1 fusion.12
  86.5 2.1 %collective-permute-start = (bf16[3,128,768]{2,1,0:T(8,128)(2,1)S(1)}, bf16[3,128,768]{2,1,0:T(8,128)(2,1)S(1)}, u32[]{:S(2)}, u32[]{:S(2)}) collective-permute-start(bf16[3,128,768]{2,1,0:T(8,128)(2,1)S(1)} %get-tuple-element.7), channel_id=1, source_target_pairs={{0,8},{8,16},{16,24},{24,32},{32,40},{40,48},{48,56},{56,64},{64,7... | collective-permute-start | bytes 1769480 | tf_op jit(solution)/shard_map/ppermute | solution.py:167
  88.6 0.0 copy-start.4
  88.6 2.4 %collective-permute-start.1 = (bf16[3,128,768]{2,1,0:T(8,128)(2,1)S(1)}, bf16[3,128,768]{2,1,0:T(8,128)(2,1)S(1)}, u32[]{:S(2)}, u32[]{:S(2)}) collective-permute-start(bf16[3,128,768]{2,1,0:T(8,128)(2,1)S(1)} %get-tuple-element.8), channel_id=1, source_target_pairs={{8,0},{16,8},{24,16},{32,24},{40,32},{48,40},{56,48},{64,56},{72,6... | collective-permute-start | bytes 1769480 | tf_op jit(solution)/shard_map/ppermute | solution.py:168
  91.1 6.8 %collective-permute-done = bf16[3,128,768]{2,1,0:T(8,128)(2,1)S(1)} collective-permute-done((bf16[3,128,768]{2,1,0:T(8,128)(2,1)S(1)}, bf16[3,128,768]{2,1,0:T(8,128)(2,1)S(1)}, u32[]{:S(2)}, u32[]{:S(2)}) %collective-permute-start) | collective-permute-done | bytes 589856 | tf_op jit(solution)/shard_map/ppermute | solution.py:167
  97.9 5.5 %collective-permute-done.1 = bf16[3,128,768]{2,1,0:T(8,128)(2,1)S(1)} collective-permute-done((bf16[3,128,768]{2,1,0:T(8,128)(2,1)S(1)}, bf16[3,128,768]{2,1,0:T(8,128)(2,1)S(1)}, u32[]{:S(2)}, u32[]{:S(2)}) %collective-permute-start.1) | collective-permute-done | bytes 589856 | tf_op jit(solution)/shard_map/ppermute | solution.py:168
  103.4 0.3 pad_maximum_fusion
  103.7 0.1 fusion.11
  103.8 2.8 %collective-permute-start.2 = (bf16[14,3,768]{2,1,0:T(4,128)(2,1)S(1)}, bf16[14,3,768]{2,1,0:T(4,128)(2,1)S(1)}, u32[]{:S(2)}, u32[]{:S(2)}) collective-permute-start(bf16[14,3,768]{2,1,0:T(4,128)(2,1)S(1)} %get-tuple-element.6), channel_id=1, source_target_pairs={{0,1},{1,2},{2,3},{3,4},{4,5},{5,6},{6,7},{8,9},{9,10},{10,11},{11... | collective-permute-start | bytes 193544 | tf_op jit(solution)/shard_map/ppermute | solution.py:167
  106.7 4.8 %collective-permute-start.3 = (bf16[14,3,768]{2,1,0:T(4,128)(2,1)S(1)}, bf16[14,3,768]{2,1,0:T(4,128)(2,1)S(1)}, u32[]{:S(2)}, u32[]{:S(2)}) collective-permute-start(bf16[14,3,768]{2,1,0:T(4,128)(2,1)S(1)} %get-tuple-element.5), channel_id=1, source_target_pairs={{1,0},{2,1},{3,2},{4,3},{5,4},{6,5},{7,6},{9,8},{10,9},{11,10},{12... | collective-permute-start | bytes 193544 | tf_op jit(solution)/shard_map/ppermute | solution.py:168
  111.5 0.0 copy-done.4
  111.5 0.1 broadcast_in_dim.21
  111.6 0.7 broadcast_in_dim_reshape.3.scale_ref
  112.3 0.0 collective-permute-done.2
  112.3 2.5 %collective-permute-done.3 = bf16[14,3,768]{2,1,0:T(4,128)(2,1)S(1)} collective-permute-done((bf16[14,3,768]{2,1,0:T(4,128)(2,1)S(1)}, bf16[14,3,768]{2,1,0:T(4,128)(2,1)S(1)}, u32[]{:S(2)}, u32[]{:S(2)}) %collective-permute-start.3) | collective-permute-done | bytes 64544 | tf_op jit(solution)/shard_map/ppermute | solution.py:168
  114.8 9.1 %concatenate.7.normed_ref = bf16[14,144,768]{2,1,0:T(8,128)(2,1)} concatenate(bf16[14,5,768]{2,1,0:T(8,128)(2,1)S(1)} %broadcast_in_dim.8, bf16[14,3,768]{2,1,0:T(4,128)(2,1)S(1)} %collective-permute-done.2, bf16[14,128,768]{2,1,0:T(8,128)(2,1)S(1)} %pad_maximum_fusion, bf16[14,3,768]{2,1,0:T(4,128)(2,1)S(1)} %collective-permute-done.3, bf16[14,5,768]{2,1,0:T(8,128)(2,1)S(1)} %broadcast_in_dim.8), dimensions={1} | concatenate | bytes 6193152 | tf_op jit(solution)/shard_map/concatenate | solution.py:172
  123.8 35.5 %attend.1 = bf16[8,128,768]{2,1,0:T(8,128)(2,1)} custom-call(bf16[14,144,768]{2,1,0:T(8,128)(2,1)} %concatenate.7.normed_ref, bf16[8,128,768]{2,1,0:T(8,128)(2,1)} %bitcast.21, bf16[8,128,768]{2,1,0:T(8,128)(2,1)} %image_ref.1, bf16[768,2304]{1,0:T(8,128)(2,1)} %w_qkv_ref.1, bf16[768,768]{1,0:T(8,128)(2,1)} %w_out_ref.1, ...), custom_call_target="tpu_custom_call" | custom-call | tf_op jit(solution)/shard_map/attend/pallas_call | solution.py:145
  (8 shorter events, 0.1 us)
Async XLA Ops:
  0.0 1.3 copy-start.2
  6.9 18.7 %all-to-all-start = ((s32[128,1,16]{2,1,0:T(1,128)}), s32[128,1,16]{2,1,0:T(1,128)S(1)}, u32[]{:S(2)}, u32[]{:S(2)}) async-start(s32[128,1,16]{2,1,0:T(1,128)} %bitcast.7), calls=%async_computation | async-start | bytes 131072 | tf_op jit(solution)/shard_map/all_to_all | solution.py:204
  25.5 59.7 %copy-start.1 = (bf16[8,128,768]{2,1,0:T(8,128)(2,1)S(1)}, bf16[8,128,768]{2,1,0:T(8,128)(2,1)}, u32[]{:S(2)}) copy-start(bf16[8,128,768]{2,1,0:T(8,128)(2,1)} %image_ref.1) | copy-start | bytes 4718596
  25.5 49.1 %all-to-all-start.1 = ((bf16[128,16,768]{2,1,0:T(8,128)(2,1)}), bf16[128,16,768]{2,1,0:T(8,128)(2,1)}, u32[]{:S(2)}, u32[]{:S(2)}) async-start(bf16[128,16,768]{2,1,0:T(8,128)(2,1)} %bitcast.22), calls=%async_computation.1 | async-start | bytes 6291456 | tf_op jit(solution)/shard_map/all_to_all | solution.py:197
  35.7 50.1 %copy-start.3 = (f32[768]{0:T(1024)S(1)}, f32[768]{0:T(1024)}, u32[]{:S(2)}) copy-start(f32[768]{0:T(1024)} %param.12) | copy-start | bytes 9220
  85.2 1.2 copy-start
  86.5 11.3 %collective-permute-start = (bf16[3,128,768]{2,1,0:T(8,128)(2,1)S(1)}, bf16[3,128,768]{2,1,0:T(8,128)(2,1)S(1)}, u32[]{:S(2)}, u32[]{:S(2)}) collective-permute-start(bf16[3,128,768]{2,1,0:T(8,128)(2,1)S(1)} %get-tuple-element.7), channel_id=1, source_target_pairs={{0,8},{8,16},{16,24},{24,32},{32,40},{40,48},{48,56},{56,64},{64,7... | collective-permute-start | bytes 1769480 | tf_op jit(solution)/shard_map/ppermute | solution.py:167
  88.6 22.9 %copy-start.4 = (f32[12]{0:T(128)S(1)}, f32[12]{0:T(128)}, u32[]{:S(2)}) copy-start(f32[12]{0:T(128)} %param.15) | copy-start | bytes 148
  88.6 14.8 %collective-permute-start.1 = (bf16[3,128,768]{2,1,0:T(8,128)(2,1)S(1)}, bf16[3,128,768]{2,1,0:T(8,128)(2,1)S(1)}, u32[]{:S(2)}, u32[]{:S(2)}) collective-permute-start(bf16[3,128,768]{2,1,0:T(8,128)(2,1)S(1)} %get-tuple-element.8), channel_id=1, source_target_pairs={{8,0},{16,8},{24,16},{32,24},{40,32},{48,40},{56,48},{64,56},{72,6... | collective-permute-start | bytes 1769480 | tf_op jit(solution)/shard_map/ppermute | solution.py:168
  103.8 8.4 %collective-permute-start.2 = (bf16[14,3,768]{2,1,0:T(4,128)(2,1)S(1)}, bf16[14,3,768]{2,1,0:T(4,128)(2,1)S(1)}, u32[]{:S(2)}, u32[]{:S(2)}) collective-permute-start(bf16[14,3,768]{2,1,0:T(4,128)(2,1)S(1)} %get-tuple-element.6), channel_id=1, source_target_pairs={{0,1},{1,2},{2,3},{3,4},{4,5},{5,6},{6,7},{8,9},{9,10},{10,11},{11... | collective-permute-start | bytes 193544 | tf_op jit(solution)/shard_map/ppermute | solution.py:167
  106.7 8.1 %collective-permute-start.3 = (bf16[14,3,768]{2,1,0:T(4,128)(2,1)S(1)}, bf16[14,3,768]{2,1,0:T(4,128)(2,1)S(1)}, u32[]{:S(2)}, u32[]{:S(2)}) collective-permute-start(bf16[14,3,768]{2,1,0:T(4,128)(2,1)S(1)} %get-tuple-element.5), channel_id=1, source_target_pairs={{1,0},{2,1},{3,2},{4,3},{5,4},{6,5},{7,6},{9,8},{10,9},{11,10},{12... | collective-permute-start | bytes 193544 | tf_op jit(solution)/shard_map/ppermute | solution.py:168
where the time goes:
time: 162 us; the launch traced here: 159 us
  waiting for transfers between devices  52.3 us (32%)
  Pallas kernels  35.5 us (22%)
  local copies, waits for them, and re-layouts  35.3 us (22%)
  starting transfers between devices  33.1 us (20%)
  other arithmetic  2.94 us (2%)
    all_to_all x1, waiting for transfers between devices, local(): lax.all_to_all(send_rows.reshape(device_count, capacity, model_width), ('...  37.5 us
    pallas_call x1, Pallas kernels, attend(): pl.pallas_call(attend_kernel, out_shape=jax.ShapeDtypeStruct(image.shape,...  35.5 us
    all_to_all x1, starting transfers between devices, local(): lax.all_to_all(send_cells.reshape(device_count, capacity), ('row', 'col')...  10.7 us
    scatter x1, local copies, waits for them, and re-layouts, local(): skip.at[got_cells.reshape(-1)]  10.6 us
    all_to_all x1, starting transfers between devices, local(): lax.all_to_all(send_rows.reshape(device_count, capacity, model_width), ('...  10.2 us
    concatenate x1, local copies, waits for them, and re-layouts, extended(): return jnp.concatenate([blank, before, array, after, blank], axis=dim)  9.07 us
    ppermute x2, waiting for transfers between devices, extended(): after = lax.ppermute(first, axis, down)  8.01 us
    scatter x1, local copies, waits for them, and re-layouts, local(): send_rows = jnp.zeros((device_count * capacity, model_width), jnp.bfloat1...  7.94 us
  transfers between devices with their start and end apart: 6, of which 4 were waited for; matrix products, arithmetic and copies ran while one was open for 6% of the time, Pallas kernels for 0%

commit v1 on v0

--- a/solution.py
+++ b/solution.py
@@ -13,6 +13,10 @@
 GROUP_COLS = 16
 HEAD = 64
 QUAD = 256
+SLOTS = 16
+STRIDE = 49
+STRIDE_INVERSE = 81
+MESH = pl.DeviceIdType.MESH
 
 
 def dot(a, b):
@@ -35,12 +39,289 @@
     return jnp.concatenate(parts, axis=1)
 
 
+def flag(condition):
+    return jnp.where(condition, 1.0, 0.0).astype(jnp.bfloat16)
+
+
+def coordinates(row, col):
+    return col // 2, (col % 2) * 2 + (row // 2) % 2, row // 4, row % 2
+
+
+def place_kernel(
+    rows_ref, owner_ref, position_ref, image_ref, gain_ref,
+    own_out, skip_out, up_out, down_out, left_out, right_out,
+    send_s, got_s, cell_send_s, cell_got_s, total_s, own_s, left_s, right_s,
+    up_land, down_land, left_land, right_land,
+    send_sem, cell_send_sem, got_sems, cell_got_sems, halo_send_sems, halo_got_sems,
+):
+    n_row, n_col = lax.axis_size("row"), lax.axis_size("col")
+    n_device = n_row * n_col
+    n_held, width = rows_ref.shape
+    tile_rows, tile_cols, _ = image_ref.shape
+    n_cell = tile_rows * tile_cols
+    my_row, my_col = lax.axis_index("row"), lax.axis_index("col")
+    my_x, my_y, my_z, my_core = coordinates(my_row, my_col)
+    chunk = 16
+    chunk_slots = chunk * SLOTS
+    n_chunk = n_device // chunk
+
+    def partner(step):
+        gap = (step * STRIDE) % n_device
+        x = (my_x + gap // 32) % 4
+        y = (my_y + (gap // 8) % 4) % 4
+        z = (my_z + (gap // 2) % 4) % 4
+        core = (my_core + gap % 2) % 2
+        return (z * 4 + (y % 2) * 2 + core, x * 2 + y // 2)
+
+    up_land[...] = jnp.zeros_like(up_land)
+    down_land[...] = jnp.zeros_like(down_land)
+    left_land[...] = jnp.zeros_like(left_land)
+    right_land[...] = jnp.zeros_like(right_land)
+
+    barrier = pltpu.get_barrier_semaphore()
+
+    def greet(step, carry):
+        pl.semaphore_signal(barrier, inc=1, device_id=partner(step), device_id_type=MESH)
+        return carry
+
+    lax.fori_loop(1, n_device, greet, 0)
+
+    owner = owner_ref[...]
+    owner_row, owner_col = owner >> 3, owner & 7
+    gap_x = ((owner_col >> 1) - my_x) & 3
+    gap_y = ((owner_col & 1) * 2 + ((owner_row >> 1) & 1) - my_y) & 3
+    gap_z = ((owner_row >> 2) - my_z) & 3
+    gap_core = ((owner_row & 1) - my_core) & 1
+    order = ((((gap_x * 4 + gap_y) * 4 + gap_z) * 2 + gap_core) * STRIDE_INVERSE) & (n_device - 1)
+    holds = lax.broadcasted_iota(jnp.int32, (n_device, n_held), 0) == order
+    holds_f = jnp.where(holds, 1.0, 0.0)
+    holds_b = holds_f.astype(jnp.bfloat16)
+    earlier = jnp.zeros((n_device, n_held), jnp.float32)
+    for start in range(0, n_held, 256):
+        at = lax.broadcasted_iota(jnp.int32, (256, n_held), 0) + start
+        to = lax.broadcasted_iota(jnp.int32, (256, n_held), 1)
+        earlier = earlier + dot(holds_b[:, start : start + 256], flag(at < to))
+    rank = jnp.sum(earlier * holds_f, axis=0, keepdims=True).astype(jnp.int32)
+    slot = order * SLOTS + rank
+    code = position_ref[...] + 1
+    lane = lax.broadcasted_iota(jnp.int32, (128, n_held), 0)
+    parts = jnp.where(lane == rank, (code >> 5).astype(jnp.float32), 0.0)
+    parts = parts + jnp.where(lane == rank + SLOTS, (code & 31).astype(jnp.float32), 0.0)
+    cell_send_s[...] = dot_nt(holds_b, parts.astype(jnp.bfloat16))[:, None, :]
+
+    total_s[...] = jnp.zeros_like(total_s)
+
+    def row_copy(step):
+        return pltpu.make_async_remote_copy(
+            src_ref=send_s.at[step],
+            dst_ref=got_s.at[step],
+            send_sem=send_sem,
+            recv_sem=got_sems.at[step // chunk],
+            device_id=partner(step),
+            device_id_type=MESH,
+        )
+
+    def cell_copy(step):
+        return pltpu.make_async_remote_copy(
+            src_ref=cell_send_s.at[step],
+            dst_ref=cell_got_s.at[step],
+            send_sem=cell_send_sem,
+            recv_sem=cell_got_sems.at[step // chunk],
+            device_id=partner(step),
+            device_id_type=MESH,
+        )
+
+    def pack(index):
+        at = lax.broadcasted_iota(jnp.int32, (chunk_slots, n_held), 0) + index * chunk_slots
+        packed = dot(flag(at == slot), rows_ref[...])
+        send_s[pl.ds(index * chunk, chunk)] = packed.astype(jnp.bfloat16).reshape(
+            chunk, SLOTS, width
+        )
+
+    def send(step, carry):
+        cell_copy(step).start()
+        row_copy(step).start()
+        return carry
+
+    pack(0)
+    pl.semaphore_wait(barrier, n_device - 1)
+    pltpu.make_async_copy(send_s.at[0], got_s.at[0], got_sems.at[0]).start()
+    pltpu.make_async_copy(cell_send_s.at[0], cell_got_s.at[0], cell_got_sems.at[0]).start()
+    lax.fori_loop(1, chunk, send, 0)
+
+    def pack_step(index, carry):
+        pack(index)
+        lax.fori_loop(index * chunk, (index + 1) * chunk, send, 0)
+        return carry
+
+    lax.fori_loop(1, n_chunk, pack_step, 0)
+
+    table_at = lax.broadcasted_iota(jnp.int32, (128, chunk_slots), 0)
+    table_slot = lax.broadcasted_iota(jnp.int32, (128, chunk_slots), 1) % SLOTS
+    table = jnp.where(table_at == table_slot, 32.0, 0.0)
+    table = table + jnp.where(table_at == table_slot + SLOTS, 1.0, 0.0)
+    table = table.astype(jnp.bfloat16)
+    source_at = lax.broadcasted_iota(jnp.int32, (chunk, chunk_slots), 0)
+    source_slot = lax.broadcasted_iota(jnp.int32, (chunk, chunk_slots), 1) // SLOTS
+
+    def unpack_step(index, carry):
+        blocks = pl.ds(index * chunk, chunk)
+        pltpu.make_async_copy(
+            cell_got_s.at[blocks], cell_got_s.at[blocks], cell_got_sems.at[index]
+        ).wait()
+        codes = dot(cell_got_s[blocks].reshape(chunk, 128).astype(jnp.bfloat16), table)
+        code_row = jnp.sum(
+            jnp.where(source_at == source_slot, codes, 0.0), axis=0, keepdims=True
+        ).astype(jnp.int32)
+        cell = lax.broadcasted_iota(jnp.int32, (n_cell, chunk_slots), 0) + 1
+        chosen = flag(cell == code_row)
+        pltpu.make_async_copy(got_s.at[blocks], got_s.at[blocks], got_sems.at[index]).wait()
+        total_s[...] += dot(chosen, got_s[blocks].reshape(chunk_slots, width))
+        return carry
+
+    lax.fori_loop(0, n_chunk, unpack_step, 0)
+
+    def norm(start, count):
+        rows = slice(start * tile_cols, (start + count) * tile_cols)
+        skip = total_s[rows]
+        image = image_ref[start : start + count].astype(jnp.float32)
+        resid = image.reshape(count * tile_cols, width) + skip
+        mean = jnp.mean(resid * resid, axis=-1, keepdims=True)
+        normed = resid * lax.rsqrt(mean + 1e-06) * gain_ref[...]
+        normed = normed.astype(jnp.bfloat16).reshape(count, tile_cols, width)
+        own_s[start : start + count] = normed
+        own_out[start : start + count] = normed
+        skip_out[start : start + count] = skip.astype(jnp.bfloat16).reshape(
+            count, tile_cols, width
+        )
+
+    def halo(index, there, src, dst):
+        return pltpu.make_async_remote_copy(
+            src_ref=src,
+            dst_ref=dst,
+            send_sem=halo_send_sems.at[index],
+            recv_sem=halo_got_sems.at[index],
+            device_id=there,
+            device_id_type=MESH,
+        )
+
+    has_up, has_down = my_row > 0, my_row < n_row - 1
+    has_left, has_right = my_col > 0, my_col < n_col - 1
+    above, below = my_row - 1, my_row + 1
+    before, after = my_col - 1, my_col + 1
+    side = tile_rows * PAD
+    half = side // 2
+    top, bottom = pl.ds(0, half), pl.ds(half, half)
+    near_top, middle, near_bottom = pl.ds(0, half), pl.ds(half, side), pl.ds(half + side, half)
+    moves = (
+        (has_up, has_down, (above, my_col), own_s.at[pl.ds(0, RIM)], down_land),
+        (has_down, has_up, (below, my_col), own_s.at[pl.ds(tile_rows - RIM, RIM)], up_land),
+        (has_left, has_right, (my_row, before), left_s, right_land.at[middle]),
+        (has_right, has_left, (my_row, after), right_s, left_land.at[middle]),
+        (
+            has_up & has_left, has_down & has_right, (above, before),
+            left_s.at[top], right_land.at[near_bottom],
+        ),
+        (
+            has_up & has_right, has_down & has_left, (above, after),
+            right_s.at[top], left_land.at[near_bottom],
+        ),
+        (
+            has_down & has_left, has_up & has_right, (below, before),
+            left_s.at[bottom], right_land.at[near_top],
+        ),
+        (
+            has_down & has_right, has_up & has_left, (below, after),
+            right_s.at[bottom], left_land.at[near_top],
+        ),
+    )
+
+    def start_move(index):
+        sends, _, there, src, dst = moves[index]
+
+        @pl.when(sends)
+        def _():
+            halo(index, there, src, dst).start()
+
+    norm(0, RIM)
+    start_move(0)
+    norm(tile_rows - RIM, RIM)
+    start_move(1)
+    norm(RIM, tile_rows - 2 * RIM)
+    first = own_s[:, 0:16].astype(jnp.float32)[:, :PAD]
+    left_s[...] = first.reshape(side, width).astype(jnp.bfloat16)
+    last = own_s[:, tile_cols - 16 :].astype(jnp.float32)[:, 16 - PAD :]
+    right_s[...] = last.reshape(side, width).astype(jnp.bfloat16)
+    for index in range(2, len(moves)):
+        start_move(index)
+    for index in range(len(moves)):
+        sends, gets, there, src, dst = moves[index]
+
+        @pl.when(gets)
+        def _():
+            halo(index, there, src, dst).wait_recv()
+
+        @pl.when(sends)
+        def _():
+            halo(index, there, src, dst).wait_send()
+
+    up_out[...] = up_land[...]
+    down_out[...] = down_land[...]
+    left_out[...] = left_land[...]
+    right_out[...] = right_land[...]
+
+    others = pl.ds(1, n_device - 1)
+    pltpu.make_async_copy(send_s.at[others], got_s.at[others], send_sem).wait()
+    pltpu.make_async_copy(cell_send_s.at[others], cell_got_s.at[others], cell_send_sem).wait()
+
+
+def place(skip_rows, owner, position, image, gain):
+    tile_rows, tile_cols, width = image.shape
+    n_device = lax.axis_size("row") * lax.axis_size("col")
+    vmem = pl.BlockSpec(memory_space=pltpu.VMEM)
+    rim = (RIM, tile_cols, width)
+    side = (tile_rows * PAD, width)
+    sides = (2 * tile_rows * PAD, width)
+    shapes = (image.shape, image.shape, rim, rim, sides, sides)
+    bf16 = jnp.bfloat16
+    n_chunk = n_device // 16
+    return pl.pallas_call(
+        place_kernel,
+        out_shape=[jax.ShapeDtypeStruct(shape, bf16) for shape in shapes],
+        in_specs=[vmem] * 5,
+        out_specs=[vmem] * 6,
+        scratch_shapes=[
+            pltpu.VMEM((n_device, SLOTS, width), bf16),
+            pltpu.VMEM((n_device, SLOTS, width), bf16),
+            pltpu.VMEM((n_device, 1, 128), jnp.float32),
+            pltpu.VMEM((n_device, 1, 128), jnp.float32),
+            pltpu.VMEM((tile_rows * tile_cols, width), jnp.float32),
+            pltpu.VMEM(image.shape, bf16),
+            pltpu.VMEM(side, bf16),
+            pltpu.VMEM(side, bf16),
+            pltpu.VMEM(rim, bf16),
+            pltpu.VMEM(rim, bf16),
+            pltpu.VMEM(sides, bf16),
+            pltpu.VMEM(sides, bf16),
+            pltpu.SemaphoreType.DMA,
+            pltpu.SemaphoreType.DMA,
+            pltpu.SemaphoreType.DMA((n_chunk,)),
+            pltpu.SemaphoreType.DMA((n_chunk,)),
+            pltpu.SemaphoreType.DMA((8,)),
+            pltpu.SemaphoreType.DMA((8,)),
+        ],
+        compiler_params=pltpu.CompilerParams(
+            collective_id=0, has_side_effects=True, vmem_limit_bytes=56 << 20
+        ),
+        name="place",
+    )(skip_rows, owner, position, image, gain)
+
+
 def attend_kernel(
-    normed_ref, skip_ref, image_ref, w_qkv_ref, w_out_ref, scale_ref, out_ref,
+    own_ref, up_ref, down_ref, left_ref, right_ref, skip_ref, image_ref, w_qkv_ref, w_out_ref, scale_ref, out_ref,
     query_s, key_s, value_s, attended_s,
 ):
-    ext_rows, ext_cols, width = normed_ref.shape
-    tile_rows, tile_cols, _ = image_ref.shape
+    tile_rows, tile_cols, width = image_ref.shape
     image_rows = tile_rows * lax.axis_size("row")
     image_cols = tile_cols * lax.axis_size("col")
     row_base = lax.axis_index("row") * tile_rows
@@ -49,26 +330,37 @@
     lane_b = lax.broadcasted_iota(jnp.int32, (QUAD, QUAD), 1) // HEAD
     ones = (lane_a == lane_b).astype(jnp.float32).astype(jnp.bfloat16)
 
-    def keyval_step(step, carry):
-        x = normed_ref[pl.ds(step * 2, 2)].reshape(2 * ext_cols, width)
+    own_cols = pl.ds(PAD, tile_cols)
+
+    def keyval(x):
         keys = dot(x, w_qkv_ref[:, width : 2 * width]).astype(jnp.bfloat16)
         keys = keys.astype(jnp.float32)
         unit = keys * lax.rsqrt(head_sums(keys, ones) + 1e-06)
-        key_s[pl.ds(step * 2, 2)] = unit.astype(jnp.bfloat16).reshape(2, ext_cols, width)
         values = dot(x, w_qkv_ref[:, 2 * width :])
-        value_s[pl.ds(step * 2, 2)] = values.astype(jnp.bfloat16).reshape(2, ext_cols, width)
-        return carry
-
-    lax.fori_loop(0, ext_rows // 2, keyval_step, 0)
-
-    def query_step(step, carry):
-        x = normed_ref[pl.ds(step * 2 + RIM, 2), PAD : PAD + tile_cols]
-        queries = dot(x.reshape(2 * tile_cols, width), w_qkv_ref[:, :width])
+        return unit.astype(jnp.bfloat16), values.astype(jnp.bfloat16)
+
+    def own_step(step, carry):
+        shape = (2, tile_cols, width)
+        x = own_ref[pl.ds(step * 2, 2)].reshape(2 * tile_cols, width)
+        unit, values = keyval(x)
+        key_s[pl.ds(step * 2 + RIM, 2), own_cols] = unit.reshape(shape)
+        value_s[pl.ds(step * 2 + RIM, 2), own_cols] = values.reshape(shape)
+        queries = dot(x, w_qkv_ref[:, :width])
         unit = queries * scale_ref[...] * lax.rsqrt(head_sums(queries, ones) + 1e-06)
-        query_s[pl.ds(step * 2, 2)] = unit.astype(jnp.bfloat16).reshape(2, tile_cols, width)
-        return carry
-
-    lax.fori_loop(0, tile_rows // 2, query_step, 0)
+        query_s[pl.ds(step * 2, 2)] = unit.astype(jnp.bfloat16).reshape(shape)
+        return carry
+
+    lax.fori_loop(0, tile_rows // 2, own_step, 0)
+    for rim_ref, at in ((up_ref, 0), (down_ref, RIM + tile_rows)):
+        unit, values = keyval(rim_ref[...].reshape(RIM * tile_cols, width))
+        key_s[at : at + RIM, own_cols] = unit.reshape(RIM, tile_cols, width)
+        value_s[at : at + RIM, own_cols] = values.reshape(RIM, tile_cols, width)
+    for side_ref, at in ((left_ref, 0), (right_ref, PAD + tile_cols)):
+        unit, values = keyval(side_ref[...])
+        shape = (2 * tile_rows, PAD, width)
+        kept = slice(1, 1 + tile_rows + 2 * RIM)
+        key_s[:, at : at + PAD] = unit.reshape(shape)[kept]
+        value_s[:, at : at + PAD] = values.reshape(shape)[kept]
 
     key_rows = GROUP_ROWS + 2 * RIM
     key_cols = GROUP_COLS + 2 * PAD
@@ -139,87 +431,32 @@
     lax.fori_loop(0, tile_rows // 2, out_step, 0)
 
 
-def attend(normed, skip, image, w_qkv, w_out, scale):
+def attend(own, up, down, left, right, skip, image, w_qkv, w_out, scale):
     tile_rows, tile_cols, width = image.shape
     vmem = pl.BlockSpec(memory_space=pltpu.VMEM)
+    extended = (tile_rows + 2 * RIM, tile_cols + 2 * PAD, width)
     return pl.pallas_call(
         attend_kernel,
         out_shape=jax.ShapeDtypeStruct(image.shape, jnp.bfloat16),
-        in_specs=[vmem] * 6,
+        in_specs=[vmem] * 10,
         out_specs=vmem,
         scratch_shapes=[
             pltpu.VMEM(image.shape, jnp.bfloat16),
-            pltpu.VMEM(normed.shape, jnp.bfloat16),
-            pltpu.VMEM(normed.shape, jnp.bfloat16),
+            pltpu.VMEM(extended, jnp.bfloat16),
+            pltpu.VMEM(extended, jnp.bfloat16),
             pltpu.VMEM(image.shape, jnp.bfloat16),
         ],
         compiler_params=pltpu.CompilerParams(vmem_limit_bytes=56 << 20),
         name="attend",
-    )(normed, skip, image, w_qkv, w_out, scale)
-
-
-def extended(array, axis, dim, width, pad):
-    peers, length = (lax.axis_size(axis), array.shape[dim])
-    up = [(i, i + 1) for i in range(peers - 1)]
-    down = [(j, i) for i, j in up]
-    last = lax.slice_in_dim(array, length - width, length, axis=dim)
-    first = lax.slice_in_dim(array, 0, width, axis=dim)
-    before = lax.ppermute(last, axis, up)
-    after = lax.ppermute(first, axis, down)
-    blank = list(array.shape)
-    blank[dim] = pad - width
-    blank = jnp.zeros(blank, array.dtype)
-    return jnp.concatenate([blank, before, array, after, blank], axis=dim)
+    )(own, up, down, left, right, skip, image, w_qkv, w_out, scale)
 
 
 def local(image, skip_rows, owners, positions, gain, w_qkv, w_out, head_scale):
-    tile_rows, tile_cols, model_width = image.shape
-    device_count = lax.axis_size("row") * lax.axis_size("col")
-    rows_held = skip_rows.shape[0]
-    capacity = 2 * rows_held // device_count
-    cell_count = tile_rows * tile_cols
-    owner_ids = owners[:, 0]
-    one_hot = (owner_ids[:, None] == jnp.arange(device_count, dtype=jnp.int32)[None, :]).astype(
-        jnp.int32
+    own, skip, up, down, left, right = place(
+        skip_rows, owners.reshape(1, -1), positions.reshape(1, -1), image, gain[None, :]
     )
-    earlier = jnp.cumsum(one_hot, axis=0) - one_hot
-    row_rank = jnp.sum(earlier * one_hot, axis=1)
-    slot_index = owner_ids * capacity + row_rank
-    send_rows = (
-        jnp.zeros((device_count * capacity, model_width), jnp.bfloat16)
-        .at[slot_index]
-        .set(skip_rows)
-    )
-    send_cells = (
-        jnp.full((device_count * capacity,), cell_count, jnp.int32).at[slot_index].set(positions)
-    )
-    got_rows, got_cells = (
-        lax.all_to_all(
-            send_rows.reshape(device_count, capacity, model_width),
-            ("row", "col"),
-            split_axis=0,
-            concat_axis=0,
-            tiled=True,
-        ),
-        lax.all_to_all(
-            send_cells.reshape(device_count, capacity),
-            ("row", "col"),
-            split_axis=0,
-            concat_axis=0,
-            tiled=True,
-        ),
-    )
-    skip = jnp.zeros((cell_count, model_width), jnp.bfloat16)
-    skip = skip.at[got_cells.reshape(-1)].set(got_rows.reshape(-1, model_width), mode="drop")
-    skip = skip.reshape(tile_rows, tile_cols, model_width)
-    resid = image.astype(jnp.float32) + skip.astype(jnp.float32)
-    normed = (
-        resid * lax.rsqrt(jnp.mean(resid * resid, axis=-1, keepdims=True) + 1e-06) * gain
-    ).astype(jnp.bfloat16)
-    normed = extended(normed, "row", 0, RIM, RIM)
-    normed = extended(normed, "col", 1, RIM, PAD)
     scale = jnp.repeat(head_scale, HEAD)[None, :]
-    return attend(normed, skip, image, w_qkv, w_out, scale)
+    return attend(own, up, down, left, right, skip, image, w_qkv, w_out, scale)
 
 
 def solution(mesh):

time: 162 us -> 116 us (0.72); the launches traced: 159 us -> 116 us
  Pallas kernels: 35.5 us -> 113 us
  waiting for transfers between devices: 52.3 us -> 0 us
  starting transfers between devices: 33.1 us -> 0 us
  local copies, waits for them, and re-layouts: 35.3 us -> 2.66 us
  other arithmetic: 2.94 us -> 0 us
    pallas_call x0 -> x1, Pallas kernels: none -> 79.3 us  [place(): pl.pallas_call(place_kernel, out_shape=[jax.ShapeDtypeStruct(shape, bf16)...]
    all_to_all x2 -> x0, waiting for transfers between devices: 37.5 us -> none  [the longest x1 37.5 us: local(): lax.all_to_all(send_rows.reshape(device_count, capacity, model_width), ('...]
    scatter x3 -> x0, local copies, waits for them, and re-layouts: 23 us -> none  [the longest x1 10.6 us: local(): skip.at[got_cells.reshape(-1)]]
    all_to_all x2 -> x0, starting transfers between devices: 20.9 us -> none  [the longest x1 10.7 us: local(): lax.all_to_all(send_cells.reshape(device_count, capacity), ('row', 'col')...]
    ppermute x4 -> x0, waiting for transfers between devices: 14.8 us -> none  [the longest x2 8.01 us: extended(): after = lax.ppermute(first, axis, down)]
    ppermute x4 -> x0, starting transfers between devices: 12.2 us -> none  [the longest x2 7.28 us: extended(): after = lax.ppermute(first, axis, down)]
    concatenate x1 -> x0, local copies, waits for them, and re-layouts: 9.07 us -> none  [extended(): return jnp.concatenate([blank, before, array, after, blank], axis=dim)]
  transfers between devices with their start and end apart: 6 -> 0, of which waited for: 4 -> 0; matrix products, arithmetic and copies ran while one was open for 6% -> 0% of each run, Pallas kernels for 0% -> 0%
where the time goes in v1:
time: 116 us
  Pallas kernels  113 us (97%)
  local copies, waits for them, and re-layouts  2.66 us (2%)
    pallas_call x1, Pallas kernels, place(): pl.pallas_call(place_kernel, out_shape=[jax.ShapeDtypeStruct(shape, bf16)...  79.3 us
    pallas_call x1, Pallas kernels, attend(): pl.pallas_call(attend_kernel, out_shape=jax.ShapeDtypeStruct(image.shape,...  34.1 us

profile of v1, /device:TPU:11, one launch (start us, length us, event | category | flops | bytes accessed | tf_op | source)
XLA Modules:
  0.0 116.1 jit_solution(12062873815670509583)
XLA Ops:
  0.0 1.3 %broadcast_in_dim.6.gain_ref = f32[1,768]{1,0:T(1,128)} reshape(f32[768]{0:T(1024)} %param.12) | data formatting | bytes 6144 | tf_op jit(solution)/shard_map/broadcast_in_dim | solution.py:456
  1.3 0.7 broadcast_in_dim.7
  2.0 0.7 broadcast_in_dim_reshape.3.scale_ref
  2.7 79.3 %place.1 = (bf16[8,128,768]{2,1,0:T(8,128)(2,1)}, bf16[8,128,768]{2,1,0:T(8,128)(2,1)}, bf16[3,128,768]{2,1,0:T(8,128)(2,1)}, bf16[3,128,768]{2,1,0:T(8,128)(2,1...) custom-call(bf16[1024,768]{1,0:T(8,128)(2,1)} %rows_ref.1, s32[1,1024]{1,0:T(1,128)} %bitcast.2, ...), custom_call_target="tpu_custom_call" | custom-call | tf_op jit(solution)/shard_map/place/pallas_call | solution.py:288
  82.0 34.1 %attend.1 = bf16[8,128,768]{2,1,0:T(8,128)(2,1)} custom-call(bf16[8,128,768]{2,1,0:T(8,128)(2,1)} %get-tuple-element.11.own_ref, bf16[3,128,768]{2,1,0:T(8,128)(2,1)} %get-tuple-element.12.up_ref, bf16[3,128,768]{2,1,0:T(8,128)(2,1)} %get-tuple-element.13.down_ref, bf16[128,768]{1,0:T(8,128)(2,1)} %get-tuple-element.14.left_ref, ...), custom_call_target="tpu_custom_call" | custom-call | tf_op jit(solution)/shard_map/attend/pallas_call | solution.py:438

commit v2 on v1

v2 whole, which is shorter than its diff:
```python
import functools

import jax
import jax.numpy as jnp
from jax import lax
from jax.experimental import pallas as pl
from jax.experimental.pallas import tpu as pltpu
from jax.sharding import PartitionSpec as P

RIM = 3
PAD = 4
CHUNKS = 4
GROUP_ROWS = 4
GROUP_COLS = 16
HEAD = 64
QUAD = 256
SLOTS = 16
STRIDE = 49
STRIDE_INVERSE = 81
MESH = pl.DeviceIdType.MESH


def dot(a, b):
    return jnp.dot(a, b, preferred_element_type=jnp.float32)


def dot_nt(a, b):
    return lax.dot_general(a, b, (((1,), (1,)), ((), ())), preferred_element_type=jnp.float32)


def head_sums(x, ones):
    square = x * x
    high = square.astype(jnp.bfloat16)
    low = (square - high.astype(jnp.float32)).astype(jnp.bfloat16)
    width = x.shape[1]
    parts = []
    for start in range(0, width, QUAD):
        lanes = slice(start, start + QUAD)
        parts.append(dot(high[:, lanes], ones) + dot(low[:, lanes], ones))
    return jnp.concatenate(parts, axis=1)


def flag(condition):
    return jnp.where(condition, 1.0, 0.0).astype(jnp.bfloat16)


def coordinates(row, col):
    return col // 2, (col % 2) * 2 + (row // 2) % 2, row // 4, row % 2


def level_kernel(
    rows_ref, owner_ref, position_ref, scale_ref, gain_ref, image_ref, w_qkv_ref, w_out_ref,
    out_ref,
    send_s, got_s, cell_send_s, cell_got_s, total_s, own_s, left_s, right_s,
    up_land, down_land, left_land, right_land,
    image_s, w_qkv_s, w_out_s, query_s, key_s, value_s, attended_s, score_s,
    send_sem, cell_send_sem, got_sems, cell_got_sems, halo_send_sems, halo_got_sems, load_sems,
):
    n_row, n_col = lax.axis_size("row"), lax.axis_size("col")
    n_device = n_row * n_col
    n_held, width = rows_ref.shape
    tile_rows, tile_cols, _ = image_ref.shape
    n_cell = tile_rows * tile_cols
    my_row, my_col = lax.axis_index("row"), lax.axis_index("col")
    my_x, my_y, my_z, my_core = coordinates(my_row, my_col)
    chunk = 16
    chunk_slots = chunk * SLOTS
    n_chunk = n_device // chunk

    def partner(step):
        gap = (step * STRIDE) % n_device
        x = (my_x + gap // 32) % 4
        y = (my_y + (gap // 8) % 4) % 4
        z = (my_z + (gap // 2) % 4) % 4
        core = (my_core + gap % 2) % 2
        return (z * 4 + (y % 2) * 2 + core, x * 2 + y // 2)

    loads = [
        pltpu.make_async_copy(src, dst, load_sems.at[index])
        for index, (src, dst) in enumerate(
            ((image_ref, image_s), (w_qkv_ref, w_qkv_s), (w_out_ref, w_out_s))
        )
    ]
    loads[0].start()
    up_land[...] = jnp.zeros_like(up_land)
    down_land[...] = jnp.zeros_like(down_land)
    left_land[...] = jnp.zeros_like(left_land)
    right_land[...] = jnp.zeros_like(right_land)

    barrier = pltpu.get_barrier_semaphore()

    def greet(step, carry):
        pl.semaphore_signal(barrier, inc=1, device_id=partner(step), device_id_type=MESH)
        return carry

    lax.fori_loop(1, n_device, greet, 0)

    owner = owner_ref[...]
    owner_row, owner_col = owner >> 3, owner & 7
    gap_x = ((owner_col >> 1) - my_x) & 3
    gap_y = ((owner_col & 1) * 2 + ((owner_row >> 1) & 1) - my_y) & 3
    gap_z = ((owner_row >> 2) - my_z) & 3
    gap_core = ((owner_row & 1) - my_core) & 1
    order = ((((gap_x * 4 + gap_y) * 4 + gap_z) * 2 + gap_core) * STRIDE_INVERSE) & (n_device - 1)
    holds = lax.broadcasted_iota(jnp.int32, (n_device, n_held), 0) == order
    holds_f = jnp.where(holds, 1.0, 0.0)
    holds_b = holds_f.astype(jnp.bfloat16)
    earlier = jnp.zeros((n_device, n_held), jnp.float32)
    for start in range(0, n_held, 256):
        at = lax.broadcasted_iota(jnp.int32, (256, n_held), 0) + start
        to = lax.broadcasted_iota(jnp.int32, (256, n_held), 1)
        earlier = earlier + dot(holds_b[:, start : start + 256], flag(at < to))
    rank = jnp.sum(earlier * holds_f, axis=0, keepdims=True).astype(jnp.int32)
    slot = order * SLOTS + rank
    code = position_ref[...] + 1
    lane = lax.broadcasted_iota(jnp.int32, (128, n_held), 0)
    parts = jnp.where(lane == rank, (code >> 5).astype(jnp.float32), 0.0)
    parts = parts + jnp.where(lane == rank + SLOTS, (code & 31).astype(jnp.float32), 0.0)
    cell_send_s[...] = dot_nt(holds_b, parts.astype(jnp.bfloat16))[:, None, :]


    def row_copy(step):
        return pltpu.make_async_remote_copy(
            src_ref=send_s.at[step],
            dst_ref=got_s.at[step],
            send_sem=send_sem,
            recv_sem=got_sems.at[step // chunk],
            device_id=partner(step),
            device_id_type=MESH,
        )

    def cell_copy(step):
        return pltpu.make_async_remote_copy(
            src_ref=cell_send_s.at[step],
            dst_ref=cell_got_s.at[step],
            send_sem=cell_send_sem,
            recv_sem=cell_got_sems.at[step // chunk],
            device_id=partner(step),
            device_id_type=MESH,
        )

    def pack(index):
        at = lax.broadcasted_iota(jnp.int32, (chunk_slots, n_held), 0) + index * chunk_slots
        packed = dot(flag(at == slot), rows_ref[...])
        send_s[pl.ds(index * chunk, chunk)] = packed.astype(jnp.bfloat16).reshape(
            chunk, SLOTS, width
        )

    def send(step, carry):
        cell_copy(step).start()
        row_copy(step).start()
        return carry

    pack(0)
    pl.semaphore_wait(barrier, n_device - 1)
    pltpu.make_async_copy(send_s.at[0], got_s.at[0], got_sems.at[0]).start()
    pltpu.make_async_copy(cell_send_s.at[0], cell_got_s.at[0], cell_got_sems.at[0]).start()
    lax.fori_loop(1, chunk, send, 0)

    def pack_step(index, carry):
        pack(index)
        lax.fori_loop(index * chunk, (index + 1) * chunk, send, 0)
        return carry

    lax.fori_loop(1, n_chunk, pack_step, 0)
    loads[0].wait()
    loads[1].start()
    loads[2].start()

    def fill_step(row, carry):
        rows = pl.ds(pl.multiple_of(row * tile_cols, tile_cols), tile_cols)
        total_s[rows] = image_s[row].astype(jnp.float32)
        return carry

    lax.fori_loop(0, tile_rows, fill_step, 0)

    table_at = lax.broadcasted_iota(jnp.int32, (128, chunk_slots), 0)
    table_slot = lax.broadcasted_iota(jnp.int32, (128, chunk_slots), 1) % SLOTS
    table = jnp.where(table_at == table_slot, 32.0, 0.0)
    table = table + jnp.where(table_at == table_slot + SLOTS, 1.0, 0.0)
    table = table.astype(jnp.bfloat16)
    source_at = lax.broadcasted_iota(jnp.int32, (chunk, chunk_slots), 0)
    source_slot = lax.broadcasted_iota(jnp.int32, (chunk, chunk_slots), 1) // SLOTS

    def unpack_step(index, carry):
        blocks = pl.ds(index * chunk, chunk)
        pltpu.make_async_copy(
            cell_got_s.at[blocks], cell_got_s.at[blocks], cell_got_sems.at[index]
        ).wait()
        codes = dot(cell_got_s[blocks].reshape(chunk, 128).astype(jnp.bfloat16), table)
        code_row = jnp.sum(
            jnp.where(source_at == source_slot, codes, 0.0), axis=0, keepdims=True
        ).astype(jnp.int32)
        cell = lax.broadcasted_iota(jnp.int32, (n_cell, chunk_slots), 0) + 1
        chosen = flag(cell == code_row)
        pltpu.make_async_copy(got_s.at[blocks], got_s.at[blocks], got_sems.at[index]).wait()
        total_s[...] += dot(chosen, got_s[blocks].reshape(chunk_slots, width))
        return carry

    lax.fori_loop(0, n_chunk, unpack_step, 0)

    def norm(start, count):
        resid = total_s[start * tile_cols : (start + count) * tile_cols]
        mean = jnp.mean(resid * resid, axis=-1, keepdims=True)
        normed = resid * lax.rsqrt(mean + 1e-06) * gain_ref[...]
        own_s[start : start + count] = normed.astype(jnp.bfloat16).reshape(
            count, tile_cols, width
        )

    def halo(index, there, src, dst):
        return pltpu.make_async_remote_copy(
            src_ref=src,
            dst_ref=dst,
            send_sem=halo_send_sems.at[index],
            recv_sem=halo_got_sems.at[index],
            device_id=there,
            device_id_type=MESH,
        )

    has_up, has_down = my_row > 0, my_row < n_row - 1
    has_left, has_right = my_col > 0, my_col < n_col - 1
    above, below = my_row - 1, my_row + 1
    before, after = my_col - 1, my_col + 1
    side = tile_rows * PAD
    half = side // 2
    top, bottom = pl.ds(0, half), pl.ds(half, half)
    near_top, middle, near_bottom = pl.ds(0, half), pl.ds(half, side), pl.ds(half + side, half)
    moves = []
    chunk_cols = tile_cols // CHUNKS
    for sends, gets, there, at, land in (
        (has_up, has_down, (above, my_col), 0, down_land),
        (has_down, has_up, (below, my_col), tile_rows - RIM, up_land),
    ):
        for index in range(CHUNKS):
            cols = pl.ds(index * chunk_cols, chunk_cols)
            moves.append((sends, gets, there, own_s.at[pl.ds(at, RIM), cols], land.at[index]))
    moves += [
        (has_left, has_right, (my_row, before), left_s, right_land.at[middle]),
        (has_right, has_left, (my_row, after), right_s, left_land.at[middle]),
        (
            has_up & has_left, has_down & has_right, (above, before),
            left_s.at[top], right_land.at[near_bottom],
        ),
        (
            has_up & has_right, has_down & has_left, (above, after),
            right_s.at[top], left_land.at[near_bottom],
        ),
        (
            has_down & has_left, has_up & has_right, (below, before),
            left_s.at[bottom], right_land.at[near_top],
        ),
        (
            has_down & has_right, has_up & has_left, (below, after),
            right_s.at[bottom], left_land.at[near_top],
        ),
    ]

    def start_move(index):
        sends, _, there, src, dst = moves[index]

        @pl.when(sends)
        def _():
            halo(index, there, src, dst).start()

    def end_move(index):
        _, gets, there, src, dst = moves[index]

        @pl.when(gets)
        def _():
            halo(index, there, src, dst).wait_recv()

    norm(0, RIM)
    start_move(0)
    start_move(1)
    norm(tile_rows - RIM, RIM)
    start_move(CHUNKS)
    start_move(CHUNKS + 1)
    norm(RIM, tile_rows - 2 * RIM)
    edge = 16
    pick_at = lax.broadcasted_iota(jnp.int32, (side, tile_rows * edge), 0)
    pick_from = lax.broadcasted_iota(jnp.int32, (side, tile_rows * edge), 1)
    pick_row, pick_col = pick_at // PAD, pick_at % PAD
    pick = flag((pick_from // edge == pick_row) & (pick_from % edge == pick_col))
    first = dot(pick, own_s[:, :edge].reshape(tile_rows * edge, width))
    left_s[...] = first.astype(jnp.bfloat16)
    pick_col = pick_col + edge - PAD
    pick = flag((pick_from // edge == pick_row) & (pick_from % edge == pick_col))
    last = dot(pick, own_s[:, tile_cols - edge :].reshape(tile_rows * edge, width))
    right_s[...] = last.astype(jnp.bfloat16)
    for index in range(2 * CHUNKS, len(moves)):
        start_move(index)
    for index in range(2, CHUNKS):
        start_move(index)
        start_move(CHUNKS + index)

    loads[1].wait()
    lane_a = lax.broadcasted_iota(jnp.int32, (QUAD, QUAD), 0) // HEAD
    lane_b = lax.broadcasted_iota(jnp.int32, (QUAD, QUAD), 1) // HEAD
    ones = flag(lane_a == lane_b)
    head_at = lax.broadcasted_iota(jnp.int32, (1, width), 1) // HEAD
    scale = jnp.zeros((1, width), jnp.float32)
    for head in range(width // HEAD):
        scale = jnp.where(head_at == head, scale_ref[head], scale)

    def keyval(x):
        keys = dot(x, w_qkv_s[:, width : 2 * width]).astype(jnp.bfloat16)
        keys = keys.astype(jnp.float32)
        unit = keys * lax.rsqrt(head_sums(keys, ones) + 1e-06)
        values = dot(x, w_qkv_s[:, 2 * width :])
        return unit, values

    own_cols = slice(PAD, PAD + tile_cols)

    def own_step(step, carry):
        shape = (2, tile_cols, width)
        x = own_s[pl.ds(step * 2, 2)].reshape(2 * tile_cols, width)
        unit, values = keyval(x)
        key_s[pl.ds(step * 2 + RIM, 2), own_cols] = unit.reshape(shape)
        value_s[pl.ds(step * 2 + RIM, 2), own_cols] = values.reshape(shape)
        queries = dot(x, w_qkv_s[:, :width])
        unit = queries * scale * lax.rsqrt(head_sums(queries, ones) + 1e-06)
        query_s[pl.ds(step * 2, 2)] = unit.astype(jnp.bfloat16).reshape(shape)
        return carry

    lax.fori_loop(0, tile_rows // 2, own_step, 0)

    def rim_step(index):
        end_move(index)
        end_move(CHUNKS + index)
        n_rim = RIM * chunk_cols
        x = jnp.concatenate(
            [up_land[index].reshape(n_rim, width), down_land[index].reshape(n_rim, width)], axis=0
        )
        unit, values = keyval(x)
        shape = (RIM, chunk_cols, width)
        cols = slice(PAD + index * chunk_cols, PAD + (index + 1) * chunk_cols)
        for at, part in ((0, slice(0, n_rim)), (RIM + tile_rows, slice(n_rim, 2 * n_rim))):
            key_s[at : at + RIM, cols] = unit[part].reshape(shape)
            value_s[at : at + RIM, cols] = values[part].reshape(shape)

    def side_step():
        for index in range(2 * CHUNKS, len(moves)):
            end_move(index)
        n_side = 2 * side
        at = lax.broadcasted_iota(jnp.int32, (2 * n_side, 2 * n_side), 0)
        source = lax.broadcasted_iota(jnp.int32, (2 * n_side, 2 * n_side), 1)
        spot = at % (2 * PAD)
        wanted = (spot // PAD) * n_side + (at // (2 * PAD)) * PAD + spot % PAD
        x = jnp.concatenate([left_land[...], right_land[...]], axis=0)
        x = dot(flag(source == wanted), x).astype(jnp.bfloat16)
        unit, values = keyval(x)
        n_ext = tile_rows + 2 * RIM
        is_left = lax.broadcasted_iota(jnp.int32, (n_ext, 2 * PAD, width), 1) < PAD
        left_cols, right_cols = slice(0, 2 * PAD), slice(tile_cols, tile_cols + 2 * PAD)
        for ref, new in ((key_s, unit), (value_s, values)):
            new = new.reshape(2 * tile_rows, 2 * PAD, width)[1 : 1 + n_ext]
            ref[:, left_cols] = jnp.where(is_left, new, ref[:, left_cols])
            ref[:, right_cols] = jnp.where(is_left, ref[:, right_cols], new)

    image_rows, image_cols = tile_rows * n_row, tile_cols * n_col
    row_base, col_base = my_row * tile_rows, my_col * tile_cols
    key_rows = GROUP_ROWS + 2 * RIM
    key_cols = GROUP_COLS + 2 * PAD
    n_query = GROUP_ROWS * GROUP_COLS
    n_key = key_rows * key_cols
    col_groups = tile_cols // GROUP_COLS
    query_at = lax.broadcasted_iota(jnp.int32, (n_query, n_key), 0)
    key_at = lax.broadcasted_iota(jnp.int32, (n_query, n_key), 1)
    key_row_at, key_col_at = key_at // key_cols, key_at % key_cols
    row_gap = key_row_at - query_at // GROUP_COLS
    col_gap = key_col_at - query_at % GROUP_COLS
    near = (
        (row_gap >= 0)
        & (row_gap <= 2 * RIM)
        & (col_gap >= PAD - RIM)
        & (col_gap <= PAD + RIM)
    )
    lane_head = lax.broadcasted_iota(jnp.int32, (1, QUAD), 1) // HEAD
    heads = QUAD // HEAD
    masks = [flag(lane_head == head) for head in range(heads)]
    quads = range(0, width, QUAD)

    def window(ref, band, col_at, lanes):
        rows = slice(band * GROUP_ROWS, band * GROUP_ROWS + key_rows)
        block = ref[rows, pl.ds(col_at, key_cols), lanes]
        return block.reshape(n_key, QUAD).astype(jnp.bfloat16)

    def score(band, group):
        col_at = pl.multiple_of(group * GROUP_COLS, GROUP_COLS)
        rows = slice(band * GROUP_ROWS, (band + 1) * GROUP_ROWS)
        for index, start in enumerate(quads):
            lanes = slice(start, start + QUAD)
            query = query_s[rows, pl.ds(col_at, GROUP_COLS), lanes].reshape(n_query, QUAD)
            spread = jnp.concatenate([query * mask for mask in masks], axis=0)
            score_s[band, index] = dot_nt(spread, window(key_s, band, col_at, lanes))

    def mix(band, group):
        col_at = pl.multiple_of(group * GROUP_COLS, GROUP_COLS)
        rows = slice(band * GROUP_ROWS, (band + 1) * GROUP_ROWS)
        key_row = row_base + band * GROUP_ROWS - RIM + key_row_at
        key_col = col_base + col_at - PAD + key_col_at
        inside = (
            near & (key_row >= 0) & (key_row < image_rows) & (key_col >= 0) & (key_col < image_cols)
        )
        bias = jnp.where(inside, 0.0, -1e30)
        for index, start in enumerate(quads):
            lanes = slice(start, start + QUAD)
            scores = score_s[band, index].reshape(heads, n_query, n_key) + bias[None]
            scores = scores.reshape(heads * n_query, n_key)
            top = jnp.max(scores, axis=1, keepdims=True)
            expo = jnp.exp(scores - top)
            inverse = 1.0 / jnp.sum(expo, axis=1, keepdims=True)
            weights = (expo * inverse).astype(jnp.bfloat16)
            mixed = dot(weights, window(value_s, band, col_at, lanes))
            joined = mixed[:n_query]
            for h in range(1, heads):
                part = mixed[h * n_query : (h + 1) * n_query]
                joined = jnp.where(lane_head == h, part, joined)
            attended_s[rows, pl.ds(col_at, GROUP_COLS), lanes] = joined.astype(
                jnp.bfloat16
            ).reshape(GROUP_ROWS, GROUP_COLS, QUAD)

    bands = tile_rows // GROUP_ROWS

    def attend(first, end):
        score(0, first)

        def step(group, carry):
            for band in range(bands):
                if band + 1 < bands:
                    score(band + 1, group)
                else:
                    score(0, jnp.minimum(group + 1, col_groups - 1))
                mix(band, group)
            return carry

        lax.fori_loop(first, end, step, 0)

    rim_step(0)
    rim_step(1)
    side_step()
    attend(0, 3)
    rim_step(2)
    attend(3, 5)
    rim_step(3)
    attend(5, col_groups)

    loads[2].wait()

    def out_step(step, carry):
        rows = pl.ds(step * 2, 2)
        flat = pl.ds(pl.multiple_of(step * 2 * tile_cols, 2 * tile_cols), 2 * tile_cols)
        projected = dot(attended_s[rows].reshape(2 * tile_cols, width), w_out_s[...])
        level = (total_s[flat] + projected).astype(jnp.bfloat16)
        out_ref[rows] = level.reshape(2, tile_cols, width)
        return carry

    lax.fori_loop(0, tile_rows // 2, out_step, 0)

    for index, (sends, _, there, src, dst) in enumerate(moves):

        @pl.when(sends)
        def _():
            halo(index, there, src, dst).wait_send()

    others = pl.ds(1, n_device - 1)
    pltpu.make_async_copy(send_s.at[others], got_s.at[others], send_sem).wait()
    pltpu.make_async_copy(cell_send_s.at[others], cell_got_s.at[others], cell_send_sem).wait()


def local(image, skip_rows, owners, positions, gain, w_qkv, w_out, head_scale):
    tile_rows, tile_cols, width = image.shape
    n_device = lax.axis_size("row") * lax.axis_size("col")
    vmem = pl.BlockSpec(memory_space=pltpu.VMEM)
    smem = pl.BlockSpec(memory_space=pltpu.SMEM)
    far = pl.BlockSpec(memory_space=pl.ANY)
    rim = (CHUNKS, RIM, tile_cols // CHUNKS, width)
    side = (tile_rows * PAD, width)
    sides = (2 * tile_rows * PAD, width)
    extended = (tile_rows + 2 * RIM, tile_cols + 4 * PAD, width)
    n_query = GROUP_ROWS * GROUP_COLS * QUAD // HEAD
    n_key = (GROUP_ROWS + 2 * RIM) * (GROUP_COLS + 2 * PAD)
    bf16, f32 = jnp.bfloat16, jnp.float32
    n_chunk = n_device // 16
    n_move = 2 * CHUNKS + 6
    return pl.pallas_call(
        level_kernel,
        out_shape=jax.ShapeDtypeStruct(image.shape, bf16),
        in_specs=[vmem, vmem, vmem, smem, vmem, far, far, far],
        out_specs=vmem,
        scratch_shapes=[
            pltpu.VMEM((n_device, SLOTS, width), bf16),
            pltpu.VMEM((n_device, SLOTS, width), bf16),
            pltpu.VMEM((n_device, 1, 128), f32),
            pltpu.VMEM((n_device, 1, 128), f32),
            pltpu.VMEM((tile_rows * tile_cols, width), f32),
            pltpu.VMEM(image.shape, bf16),
            pltpu.VMEM(side, bf16),
            pltpu.VMEM(side, bf16),
            pltpu.VMEM(rim, bf16),
            pltpu.VMEM(rim, bf16),
            pltpu.VMEM(sides, bf16),
            pltpu.VMEM(sides, bf16),
            pltpu.VMEM(image.shape, bf16),
            pltpu.VMEM(w_qkv.shape, bf16),
            pltpu.VMEM(w_out.shape, bf16),
            pltpu.VMEM(image.shape, bf16),
            pltpu.VMEM(extended, f32),
            pltpu.VMEM(extended, f32),
            pltpu.VMEM(image.shape, bf16),
            pltpu.VMEM((tile_rows // GROUP_ROWS, width // QUAD, n_query, n_key), f32),
            pltpu.SemaphoreType.DMA,
            pltpu.SemaphoreType.DMA,
            pltpu.SemaphoreType.DMA((n_chunk,)),
            pltpu.SemaphoreType.DMA((n_chunk,)),
            pltpu.SemaphoreType.DMA((n_move,)),
            pltpu.SemaphoreType.DMA((n_move,)),
            pltpu.SemaphoreType.DMA((3,)),
        ],
        compiler_params=pltpu.CompilerParams(
            collective_id=0, has_side_effects=True, vmem_limit_bytes=60 << 20
        ),
        name="level",
    )(
        skip_rows,
        owners.reshape(1, -1),
        positions.reshape(1, -1),
        head_scale,
        gain,
        image,
        w_qkv,
        w_out,
    )


def solution(mesh):
    in_specs = (
        P("row", "col", None),
        P(("row", "col"), None),
        P(("row", "col"), None),
        P(("row", "col")),
        P(),
        P(),
        P(),
        P(),
    )
    out_specs = P("row", "col", None)
    return jax.shard_map(local, mesh=mesh, in_specs=in_specs, out_specs=out_specs, check_vma=False)
```

time: 116 us -> 84 us (0.72)
  Pallas kernels: 113 us -> 80.9 us
    pallas_call x2 -> x1, Pallas kernels: 113 us -> 80.9 us  [local(): pl.pallas_call(level_kernel, out_shape=jax.ShapeDtypeStruct(image.shape,...]
    unnamed x0 -> x1, local copies, waits for them, and re-layouts: none -> 2.65 us
    broadcast_in_dim x2 -> x0, local copies, waits for them, and re-layouts: 1.99 us -> none  [the longest x1 1.27 us: local(): gain[None, :]]
where the time goes in v2:
time: 84 us; the launch traced here: 83.6 us
  Pallas kernels  80.9 us (96%)
  local copies, waits for them, and re-layouts  2.65 us (3%)
    pallas_call x1, Pallas kernels, local(): pl.pallas_call(level_kernel, out_shape=jax.ShapeDtypeStruct(image.shape,...  80.9 us
    unnamed x1, local copies, waits for them, and re-layouts  2.65 us

profile of v2, /device:TPU:11, one launch (start us, length us, event | category | flops | bytes accessed | tf_op | source)
XLA Modules:
  0.0 83.6 jit_solution(11888430246860203040)
XLA Ops:
  0.0 80.9 %level.1 = bf16[8,128,768]{2,1,0:T(8,128)(2,1)} custom-call(bf16[1024,768]{1,0:T(8,128)(2,1)} %rows_ref.1, s32[1,1024]{1,0:T(1,128)} %bitcast.2, s32[1,1024]{1,0:T(1,128)} %bitcast.3, f32[12]{0:T(128)} %scale_ref.1, f32[768]{0:T(1024)} %gain_ref.1, bf16[8,128,768]{2,1,0:T(8,128)(2,1)} %image_ref.1, bf16[768,2304]{1,0:T(8,128)(2,1)} %w_qkv_ref.1, ...), custom_call_target="tpu_custom_call" | custom-call | tf_op jit(solution)/shard_map/level/pallas_call | solution.py:486
  80.9 2.7 %copy.10 = bf16[8,128,768]{2,1,0:T(8,128)(2,1)} copy(bf16[8,128,768]{2,1,0:T(8,128)(2,1)} %level.1) | data formatting | bytes 3145728

commit v3 on v2

--- a/solution.py
+++ b/solution.py
@@ -54,7 +54,7 @@
     send_s, got_s, cell_send_s, cell_got_s, total_s, own_s, left_s, right_s,
     up_land, down_land, left_land, right_land,
     image_s, w_qkv_s, w_out_s, query_s, key_s, value_s, attended_s, score_s,
-    send_sem, cell_send_sem, got_sems, cell_got_sems, halo_send_sems, halo_got_sems, load_sems,
+    send_sem, cell_send_sem, got_sems, cell_got_sems, halo_send_sems, halo_got_sems, load_sems, meet_sems,
 ):
     n_row, n_col = lax.axis_size("row"), lax.axis_size("col")
     n_device = n_row * n_col
@@ -67,13 +67,31 @@
     chunk_slots = chunk * SLOTS
     n_chunk = n_device // chunk
 
+    def shifted(x_gap, y_gap, z_gap, core_gap):
+        x, y, z = (my_x + x_gap) % 4, (my_y + y_gap) % 4, (my_z + z_gap) % 4
+        core = (my_core + core_gap) % 2
+        return (z * 4 + (y % 2) * 2 + core, x * 2 + y // 2)
+
     def partner(step):
         gap = (step * STRIDE) % n_device
-        x = (my_x + gap // 32) % 4
-        y = (my_y + (gap // 8) % 4) % 4
-        z = (my_z + (gap // 2) % 4) % 4
-        core = (my_core + gap % 2) % 2
-        return (z * 4 + (y % 2) * 2 + core, x * 2 + y // 2)
+        return shifted(gap // 32, (gap // 8) % 4, (gap // 2) % 4, gap % 2)
+
+    x_peers = [(gap, 0, 0, 0) for gap in range(1, 4)]
+    y_peers = [(0, gap, 0, 0) for gap in range(1, 4)]
+    z_peers = [(0, 0, gap // 2, gap % 2) for gap in range(1, 8)]
+
+    def signal(semaphore, peers):
+        for peer in peers:
+            pl.semaphore_signal(
+                semaphore, inc=1, device_id=shifted(*peer), device_id_type=MESH
+            )
+
+    up_land[...] = jnp.zeros_like(up_land)
+    down_land[...] = jnp.zeros_like(down_land)
+    left_land[...] = jnp.zeros_like(left_land)
+    right_land[...] = jnp.zeros_like(right_land)
+    barrier = pltpu.get_barrier_semaphore()
+    signal(barrier, x_peers + y_peers + z_peers)
 
     loads = [
         pltpu.make_async_copy(src, dst, load_sems.at[index])
@@ -82,18 +100,6 @@
         )
     ]
     loads[0].start()
-    up_land[...] = jnp.zeros_like(up_land)
-    down_land[...] = jnp.zeros_like(down_land)
-    left_land[...] = jnp.zeros_like(left_land)
-    right_land[...] = jnp.zeros_like(right_land)
-
-    barrier = pltpu.get_barrier_semaphore()
-
-    def greet(step, carry):
-        pl.semaphore_signal(barrier, inc=1, device_id=partner(step), device_id_type=MESH)
-        return carry
-
-    lax.fori_loop(1, n_device, greet, 0)
 
     owner = owner_ref[...]
     owner_row, owner_col = owner >> 3, owner & 7
@@ -110,6 +116,8 @@
         at = lax.broadcasted_iota(jnp.int32, (256, n_held), 0) + start
         to = lax.broadcasted_iota(jnp.int32, (256, n_held), 1)
         earlier = earlier + dot(holds_b[:, start : start + 256], flag(at < to))
+    pl.semaphore_wait(barrier, len(x_peers + y_peers + z_peers))
+    signal(meet_sems.at[0], y_peers)
     rank = jnp.sum(earlier * holds_f, axis=0, keepdims=True).astype(jnp.int32)
     slot = order * SLOTS + rank
     code = position_ref[...] + 1
@@ -151,8 +159,10 @@
         row_copy(step).start()
         return carry
 
+    pl.semaphore_wait(meet_sems.at[0], len(y_peers))
+    signal(meet_sems.at[1], z_peers)
     pack(0)
-    pl.semaphore_wait(barrier, n_device - 1)
+    pl.semaphore_wait(meet_sems.at[1], len(z_peers))
     pltpu.make_async_copy(send_s.at[0], got_s.at[0], got_sems.at[0]).start()
     pltpu.make_async_copy(cell_send_s.at[0], cell_got_s.at[0], cell_got_sems.at[0]).start()
     lax.fori_loop(1, chunk, send, 0)
@@ -516,6 +526,7 @@
             pltpu.SemaphoreType.DMA((n_move,)),
             pltpu.SemaphoreType.DMA((n_move,)),
             pltpu.SemaphoreType.DMA((3,)),
+            pltpu.SemaphoreType.REGULAR((2,)),
         ],
         compiler_params=pltpu.CompilerParams(
             collective_id=0, has_side_effects=True, vmem_limit_bytes=60 << 20

time: 84 us -> 79.5 us (0.946)
  Pallas kernels: 80.9 us -> 76.3 us
    pallas_call x1, Pallas kernels: 80.9 us -> 76.3 us  [local(): pl.pallas_call(level_kernel, out_shape=jax.ShapeDtypeStruct(image.shape,...]
where the time goes in v3:
time: 79.5 us; the launch traced here: 78.9 us
  Pallas kernels  76.3 us (96%)
  local copies, waits for them, and re-layouts  2.65 us (3%)
    pallas_call x1, Pallas kernels, local(): pl.pallas_call(level_kernel, out_shape=jax.ShapeDtypeStruct(image.shape,...  76.3 us
    unnamed x1, local copies, waits for them, and re-layouts  2.65 us

profile of v3, /device:TPU:11, one launch (start us, length us, event | category | flops | bytes accessed | tf_op | source)
XLA Modules:
  0.0 78.9 jit_solution(5088714280516841035)
XLA Ops:
  0.0 76.3 %level.1 = bf16[8,128,768]{2,1,0:T(8,128)(2,1)} custom-call(bf16[1024,768]{1,0:T(8,128)(2,1)} %rows_ref.1, s32[1,1024]{1,0:T(1,128)} %bitcast.2, s32[1,1024]{1,0:T(1,128)} %bitcast.3, f32[12]{0:T(128)} %scale_ref.1, f32[768]{0:T(1024)} %gain_ref.1, bf16[8,128,768]{2,1,0:T(8,128)(2,1)} %image_ref.1, bf16[768,2304]{1,0:T(8,128)(2,1)} %w_qkv_ref.1, ...), custom_call_target="tpu_custom_call" | custom-call | tf_op jit(solution)/shard_map/level/pallas_call | solution.py:496
  76.3 2.7 %copy.10 = bf16[8,128,768]{2,1,0:T(8,128)(2,1)} copy(bf16[8,128,768]{2,1,0:T(8,128)(2,1)} %level.1) | data formatting | bytes 3145728

commit v4 on v3

--- a/solution.py
+++ b/solution.py
@@ -10,7 +10,6 @@
 RIM = 3
 PAD = 4
 CHUNKS = 4
-GROUP_ROWS = 4
 GROUP_COLS = 16
 HEAD = 64
 QUAD = 256
@@ -31,12 +30,11 @@
 def head_sums(x, ones):
     square = x * x
     high = square.astype(jnp.bfloat16)
-    low = (square - high.astype(jnp.float32)).astype(jnp.bfloat16)
     width = x.shape[1]
     parts = []
     for start in range(0, width, QUAD):
         lanes = slice(start, start + QUAD)
-        parts.append(dot(high[:, lanes], ones) + dot(low[:, lanes], ones))
+        parts.append(dot(high[:, lanes], ones))
     return jnp.concatenate(parts, axis=1)
 
 
@@ -49,11 +47,11 @@
 
 
 def level_kernel(
-    rows_ref, owner_ref, position_ref, scale_ref, gain_ref, image_ref, w_qkv_ref, w_out_ref,
+    owner_ref, position_ref, scale_ref, gain_ref, rows_ref, image_ref, w_qkv_ref, w_out_ref,
     out_ref,
     send_s, got_s, cell_send_s, cell_got_s, total_s, own_s, left_s, right_s,
     up_land, down_land, left_land, right_land,
-    image_s, w_qkv_s, w_out_s, query_s, key_s, value_s, attended_s, score_s,
+    rows_s, image_s, w_qkv_s, w_out_s, query_s, key_s, value_s, attended_s, score_s,
     send_sem, cell_send_sem, got_sems, cell_got_sems, halo_send_sems, halo_got_sems, load_sems, meet_sems,
 ):
     n_row, n_col = lax.axis_size("row"), lax.axis_size("col")
@@ -96,9 +94,15 @@
     loads = [
         pltpu.make_async_copy(src, dst, load_sems.at[index])
         for index, (src, dst) in enumerate(
-            ((image_ref, image_s), (w_qkv_ref, w_qkv_s), (w_out_ref, w_out_s))
+            (
+                (image_ref, image_s),
+                (w_qkv_ref, w_qkv_s),
+                (w_out_ref, w_out_s),
+                (rows_ref, rows_s),
+            )
         )
     ]
+    loads[3].start()
     loads[0].start()
 
     owner = owner_ref[...]
@@ -149,7 +153,7 @@
 
     def pack(index):
         at = lax.broadcasted_iota(jnp.int32, (chunk_slots, n_held), 0) + index * chunk_slots
-        packed = dot(flag(at == slot), rows_ref[...])
+        packed = dot(flag(at == slot), rows_s[...])
         send_s[pl.ds(index * chunk, chunk)] = packed.astype(jnp.bfloat16).reshape(
             chunk, SLOTS, width
         )
@@ -161,6 +165,7 @@
 
     pl.semaphore_wait(meet_sems.at[0], len(y_peers))
     signal(meet_sems.at[1], z_peers)
+    loads[3].wait()
     pack(0)
     pl.semaphore_wait(meet_sems.at[1], len(z_peers))
     pltpu.make_async_copy(send_s.at[0], got_s.at[0], got_sems.at[0]).start()
@@ -178,8 +183,7 @@
     loads[2].start()
 
     def fill_step(row, carry):
-        rows = pl.ds(pl.multiple_of(row * tile_cols, tile_cols), tile_cols)
-        total_s[rows] = image_s[row].astype(jnp.float32)
+        total_s[row] = image_s[row].astype(jnp.float32)
         return carry
 
     lax.fori_loop(0, tile_rows, fill_step, 0)
@@ -204,13 +208,14 @@
         cell = lax.broadcasted_iota(jnp.int32, (n_cell, chunk_slots), 0) + 1
         chosen = flag(cell == code_row)
         pltpu.make_async_copy(got_s.at[blocks], got_s.at[blocks], got_sems.at[index]).wait()
-        total_s[...] += dot(chosen, got_s[blocks].reshape(chunk_slots, width))
+        found = dot(chosen, got_s[blocks].reshape(chunk_slots, width))
+        total_s[...] += found.reshape(tile_rows, tile_cols, width)
         return carry
 
     lax.fori_loop(0, n_chunk, unpack_step, 0)
 
     def norm(start, count):
-        resid = total_s[start * tile_cols : (start + count) * tile_cols]
+        resid = total_s[start : start + count].reshape(count * tile_cols, width)
         mean = jnp.mean(resid * resid, axis=-1, keepdims=True)
         normed = resid * lax.rsqrt(mean + 1e-06) * gain_ref[...]
         own_s[start : start + count] = normed.astype(jnp.bfloat16).reshape(
@@ -236,14 +241,18 @@
     top, bottom = pl.ds(0, half), pl.ds(half, half)
     near_top, middle, near_bottom = pl.ds(0, half), pl.ds(half, side), pl.ds(half + side, half)
     moves = []
-    chunk_cols = tile_cols // CHUNKS
+    part = tile_cols // 4
+    bounds = (0, part, 2 * part, 3 * part, tile_cols)
+    spans = [(bounds[index], bounds[index + 1] - bounds[index]) for index in range(CHUNKS)]
     for sends, gets, there, at, land in (
         (has_up, has_down, (above, my_col), 0, down_land),
         (has_down, has_up, (below, my_col), tile_rows - RIM, up_land),
     ):
         for index in range(CHUNKS):
-            cols = pl.ds(index * chunk_cols, chunk_cols)
-            moves.append((sends, gets, there, own_s.at[pl.ds(at, RIM), cols], land.at[index]))
+            cols = pl.ds(*spans[index])
+            moves.append(
+                (sends, gets, there, own_s.at[pl.ds(at, RIM), cols], land.at[:, cols])
+            )
     moves += [
         (has_left, has_right, (my_row, before), left_s, right_land.at[middle]),
         (has_right, has_left, (my_row, after), right_s, left_land.at[middle]),
@@ -286,6 +295,8 @@
     start_move(CHUNKS)
     start_move(CHUNKS + 1)
     norm(RIM, tile_rows - 2 * RIM)
+    start_move(2)
+    start_move(CHUNKS + 2)
     edge = 16
     pick_at = lax.broadcasted_iota(jnp.int32, (side, tile_rows * edge), 0)
     pick_from = lax.broadcasted_iota(jnp.int32, (side, tile_rows * edge), 1)
@@ -299,7 +310,7 @@
     right_s[...] = last.astype(jnp.bfloat16)
     for index in range(2 * CHUNKS, len(moves)):
         start_move(index)
-    for index in range(2, CHUNKS):
+    for index in range(3, CHUNKS):
         start_move(index)
         start_move(CHUNKS + index)
 
@@ -320,30 +331,33 @@
         return unit, values
 
     own_cols = slice(PAD, PAD + tile_cols)
+    batch = tile_rows // 2
 
     def own_step(step, carry):
-        shape = (2, tile_cols, width)
-        x = own_s[pl.ds(step * 2, 2)].reshape(2 * tile_cols, width)
+        shape = (batch, tile_cols, width)
+        x = own_s[pl.ds(step * batch, batch)].reshape(batch * tile_cols, width)
         unit, values = keyval(x)
-        key_s[pl.ds(step * 2 + RIM, 2), own_cols] = unit.reshape(shape)
-        value_s[pl.ds(step * 2 + RIM, 2), own_cols] = values.reshape(shape)
+        key_s[pl.ds(step * batch + RIM, batch), own_cols] = unit.reshape(shape)
+        value_s[pl.ds(step * batch + RIM, batch), own_cols] = values.reshape(shape)
         queries = dot(x, w_qkv_s[:, :width])
         unit = queries * scale * lax.rsqrt(head_sums(queries, ones) + 1e-06)
-        query_s[pl.ds(step * 2, 2)] = unit.astype(jnp.bfloat16).reshape(shape)
+        query_s[pl.ds(step * batch, batch)] = unit.astype(jnp.bfloat16).reshape(shape)
         return carry
 
-    lax.fori_loop(0, tile_rows // 2, own_step, 0)
+    lax.fori_loop(0, tile_rows // batch, own_step, 0)
 
     def rim_step(index):
         end_move(index)
         end_move(CHUNKS + index)
+        at_col, chunk_cols = spans[index]
+        taken = slice(at_col, at_col + chunk_cols)
         n_rim = RIM * chunk_cols
         x = jnp.concatenate(
-            [up_land[index].reshape(n_rim, width), down_land[index].reshape(n_rim, width)], axis=0
+            [land[:, taken].reshape(n_rim, width) for land in (up_land, down_land)], axis=0
         )
         unit, values = keyval(x)
         shape = (RIM, chunk_cols, width)
-        cols = slice(PAD + index * chunk_cols, PAD + (index + 1) * chunk_cols)
+        cols = slice(PAD + at_col, PAD + at_col + chunk_cols)
         for at, part in ((0, slice(0, n_rim)), (RIM + tile_rows, slice(n_rim, 2 * n_rim))):
             key_s[at : at + RIM, cols] = unit[part].reshape(shape)
             value_s[at : at + RIM, cols] = values[part].reshape(shape)
@@ -369,103 +383,130 @@
 
     image_rows, image_cols = tile_rows * n_row, tile_cols * n_col
     row_base, col_base = my_row * tile_rows, my_col * tile_cols
-    key_rows = GROUP_ROWS + 2 * RIM
     key_cols = GROUP_COLS + 2 * PAD
-    n_query = GROUP_ROWS * GROUP_COLS
-    n_key = key_rows * key_cols
     col_groups = tile_cols // GROUP_COLS
-    query_at = lax.broadcasted_iota(jnp.int32, (n_query, n_key), 0)
-    key_at = lax.broadcasted_iota(jnp.int32, (n_query, n_key), 1)
-    key_row_at, key_col_at = key_at // key_cols, key_at % key_cols
-    row_gap = key_row_at - query_at // GROUP_COLS
-    col_gap = key_col_at - query_at % GROUP_COLS
-    near = (
-        (row_gap >= 0)
-        & (row_gap <= 2 * RIM)
-        & (col_gap >= PAD - RIM)
-        & (col_gap <= PAD + RIM)
-    )
     lane_head = lax.broadcasted_iota(jnp.int32, (1, QUAD), 1) // HEAD
     heads = QUAD // HEAD
     masks = [flag(lane_head == head) for head in range(heads)]
     quads = range(0, width, QUAD)
 
+    def shape_of(count):
+        n_query, n_key = count * GROUP_COLS, (count + 2 * RIM) * key_cols
+        query_at = lax.broadcasted_iota(jnp.int32, (n_query, n_key), 0)
+        key_at = lax.broadcasted_iota(jnp.int32, (n_query, n_key), 1)
+        key_row_at, key_col_at = key_at // key_cols, key_at % key_cols
+        row_gap = key_row_at - query_at // GROUP_COLS
+        col_gap = key_col_at - query_at % GROUP_COLS
+        near = (
+            (row_gap >= 0)
+            & (row_gap <= 2 * RIM)
+            & (col_gap >= PAD - RIM)
+            & (col_gap <= PAD + RIM)
+        )
+        return n_query, n_key, key_row_at, key_col_at, near
+
+    n_middle = tile_rows - 2 * RIM
+    shapes = {RIM: shape_of(RIM), n_middle: shape_of(n_middle)}
+    upper, middle_band, lower = (0, RIM), (RIM, n_middle), (tile_rows - RIM, RIM)
+
     def window(ref, band, col_at, lanes):
-        rows = slice(band * GROUP_ROWS, band * GROUP_ROWS + key_rows)
-        block = ref[rows, pl.ds(col_at, key_cols), lanes]
-        return block.reshape(n_key, QUAD).astype(jnp.bfloat16)
-
-    def score(band, group):
-        col_at = pl.multiple_of(group * GROUP_COLS, GROUP_COLS)
-        rows = slice(band * GROUP_ROWS, (band + 1) * GROUP_ROWS)
-        for index, start in enumerate(quads):
-            lanes = slice(start, start + QUAD)
-            query = query_s[rows, pl.ds(col_at, GROUP_COLS), lanes].reshape(n_query, QUAD)
+        start, count = band
+        block = ref[start : start + count + 2 * RIM, pl.ds(col_at, key_cols), lanes]
+        return block.reshape(-1, QUAD).astype(jnp.bfloat16)
+
+    def column(group):
+        return pl.multiple_of(group * GROUP_COLS, GROUP_COLS)
+
+    def score(band, group, slot):
+        start, count = band
+        n_query, n_key, _, _, _ = shapes[count]
+        col_at = column(group)
+        for index, at in enumerate(quads):
+            lanes = slice(at, at + QUAD)
+            query = query_s[start : start + count, pl.ds(col_at, GROUP_COLS), lanes]
+            query = query.reshape(n_query, QUAD)
             spread = jnp.concatenate([query * mask for mask in masks], axis=0)
-            score_s[band, index] = dot_nt(spread, window(key_s, band, col_at, lanes))
-
-    def mix(band, group):
-        col_at = pl.multiple_of(group * GROUP_COLS, GROUP_COLS)
-        rows = slice(band * GROUP_ROWS, (band + 1) * GROUP_ROWS)
-        key_row = row_base + band * GROUP_ROWS - RIM + key_row_at
+            score_s[slot, index, : heads * n_query, :n_key] = dot_nt(
+                spread, window(key_s, band, col_at, lanes)
+            )
+
+    def mix(band, group, slot):
+        start, count = band
+        n_query, n_key, key_row_at, key_col_at, near = shapes[count]
+        col_at = column(group)
+        key_row = row_base + start - RIM + key_row_at
         key_col = col_base + col_at - PAD + key_col_at
         inside = (
             near & (key_row >= 0) & (key_row < image_rows) & (key_col >= 0) & (key_col < image_cols)
         )
         bias = jnp.where(inside, 0.0, -1e30)
-        for index, start in enumerate(quads):
-            lanes = slice(start, start + QUAD)
-            scores = score_s[band, index].reshape(heads, n_query, n_key) + bias[None]
+        for index, at in enumerate(quads):
+            lanes = slice(at, at + QUAD)
+            scores = score_s[slot, index, : heads * n_query, :n_key]
+            scores = scores.reshape(heads, n_query, n_key) + bias[None]
             scores = scores.reshape(heads * n_query, n_key)
             top = jnp.max(scores, axis=1, keepdims=True)
             expo = jnp.exp(scores - top)
             inverse = 1.0 / jnp.sum(expo, axis=1, keepdims=True)
-            weights = (expo * inverse).astype(jnp.bfloat16)
-            mixed = dot(weights, window(value_s, band, col_at, lanes))
+            mixed = dot(expo.astype(jnp.bfloat16), window(value_s, band, col_at, lanes))
+            mixed = mixed * inverse
             joined = mixed[:n_query]
             for h in range(1, heads):
                 part = mixed[h * n_query : (h + 1) * n_query]
                 joined = jnp.where(lane_head == h, part, joined)
-            attended_s[rows, pl.ds(col_at, GROUP_COLS), lanes] = joined.astype(
+            attended_s[start : start + count, pl.ds(col_at, GROUP_COLS), lanes] = joined.astype(
                 jnp.bfloat16
-            ).reshape(GROUP_ROWS, GROUP_COLS, QUAD)
-
-    bands = tile_rows // GROUP_ROWS
+            ).reshape(count, GROUP_COLS, QUAD)
+
+    def attend_middle(first, end):
+        score(middle_band, first, 0)
+
+        def step(index, carry):
+            group = first + 2 * index
+            score(middle_band, group + 1, 1)
+            mix(middle_band, group, 0)
+            score(middle_band, jnp.minimum(group + 2, col_groups - 1), 0)
+            mix(middle_band, group + 1, 1)
+            return carry
+
+        lax.fori_loop(0, (end - first) // 2, step, 0)
 
     def attend(first, end):
-        score(0, first)
+        score(upper, first, 0)
 
         def step(group, carry):
-            for band in range(bands):
-                if band + 1 < bands:
-                    score(band + 1, group)
-                else:
-                    score(0, jnp.minimum(group + 1, col_groups - 1))
-                mix(band, group)
+            score(lower, group, 1)
+            mix(upper, group, 0)
+            score(upper, jnp.minimum(group + 1, col_groups - 1), 0)
+            mix(lower, group, 1)
             return carry
 
         lax.fori_loop(first, end, step, 0)
 
+    def project(first, end):
+        cols = slice(first * GROUP_COLS, end * GROUP_COLS)
+        flat = tile_rows * (end - first) * GROUP_COLS
+        projected = dot(attended_s[:, cols].reshape(flat, width), w_out_s[...])
+        level = total_s[:, cols] + projected.reshape(tile_rows, -1, width)
+        out_ref[:, cols] = level.astype(jnp.bfloat16)
+
+    attend_middle(1, col_groups - 1)
     rim_step(0)
     rim_step(1)
-    side_step()
-    attend(0, 3)
+    attend(1, 3)
     rim_step(2)
     attend(3, 5)
+    side_step()
+    score(middle_band, 0, 0)
+    score(middle_band, col_groups - 1, 1)
+    mix(middle_band, 0, 0)
+    mix(middle_band, col_groups - 1, 1)
+    attend(0, 1)
+    loads[2].wait()
+    project(0, 5)
     rim_step(3)
     attend(5, col_groups)
-
-    loads[2].wait()
-
-    def out_step(step, carry):
-        rows = pl.ds(step * 2, 2)
-        flat = pl.ds(pl.multiple_of(step * 2 * tile_cols, 2 * tile_cols), 2 * tile_cols)
-        projected = dot(attended_s[rows].reshape(2 * tile_cols, width), w_out_s[...])
-        level = (total_s[flat] + projected).astype(jnp.bfloat16)
-        out_ref[rows] = level.reshape(2, tile_cols, width)
-        return carry
-
-    lax.fori_loop(0, tile_rows // 2, out_step, 0)
+    project(5, col_groups)
 
     for index, (sends, _, there, src, dst) in enumerate(moves):
 
@@ -484,26 +525,26 @@
     vmem = pl.BlockSpec(memory_space=pltpu.VMEM)
     smem = pl.BlockSpec(memory_space=pltpu.SMEM)
     far = pl.BlockSpec(memory_space=pl.ANY)
-    rim = (CHUNKS, RIM, tile_cols // CHUNKS, width)
+    rim = (RIM, tile_cols, width)
     side = (tile_rows * PAD, width)
     sides = (2 * tile_rows * PAD, width)
     extended = (tile_rows + 2 * RIM, tile_cols + 4 * PAD, width)
-    n_query = GROUP_ROWS * GROUP_COLS * QUAD // HEAD
-    n_key = (GROUP_ROWS + 2 * RIM) * (GROUP_COLS + 2 * PAD)
+    n_query = RIM * GROUP_COLS * QUAD // HEAD
+    n_key = 3 * RIM * (GROUP_COLS + 2 * PAD)
     bf16, f32 = jnp.bfloat16, jnp.float32
     n_chunk = n_device // 16
     n_move = 2 * CHUNKS + 6
     return pl.pallas_call(
         level_kernel,
         out_shape=jax.ShapeDtypeStruct(image.shape, bf16),
-        in_specs=[vmem, vmem, vmem, smem, vmem, far, far, far],
+        in_specs=[vmem, vmem, smem, vmem, far, far, far, far],
         out_specs=vmem,
         scratch_shapes=[
             pltpu.VMEM((n_device, SLOTS, width), bf16),
             pltpu.VMEM((n_device, SLOTS, width), bf16),
             pltpu.VMEM((n_device, 1, 128), f32),
             pltpu.VMEM((n_device, 1, 128), f32),
-            pltpu.VMEM((tile_rows * tile_cols, width), f32),
+            pltpu.VMEM(image.shape, f32),
             pltpu.VMEM(image.shape, bf16),
             pltpu.VMEM(side, bf16),
             pltpu.VMEM(side, bf16),
@@ -511,6 +552,7 @@
             pltpu.VMEM(rim, bf16),
             pltpu.VMEM(sides, bf16),
             pltpu.VMEM(sides, bf16),
+            pltpu.VMEM(skip_rows.shape, bf16),
             pltpu.VMEM(image.shape, bf16),
             pltpu.VMEM(w_qkv.shape, bf16),
             pltpu.VMEM(w_out.shape, bf16),
@@ -518,14 +560,14 @@
             pltpu.VMEM(extended, f32),
             pltpu.VMEM(extended, f32),
             pltpu.VMEM(image.shape, bf16),
-            pltpu.VMEM((tile_rows // GROUP_ROWS, width // QUAD, n_query, n_key), f32),
+            pltpu.VMEM((2, width // QUAD, n_query, n_key), f32),
             pltpu.SemaphoreType.DMA,
             pltpu.SemaphoreType.DMA,
             pltpu.SemaphoreType.DMA((n_chunk,)),
             pltpu.SemaphoreType.DMA((n_chunk,)),
             pltpu.SemaphoreType.DMA((n_move,)),
             pltpu.SemaphoreType.DMA((n_move,)),
-            pltpu.SemaphoreType.DMA((3,)),
+            pltpu.SemaphoreType.DMA((4,)),
             pltpu.SemaphoreType.REGULAR((2,)),
         ],
         compiler_params=pltpu.CompilerParams(
@@ -533,11 +575,11 @@
         ),
         name="level",
     )(
-        skip_rows,
         owners.reshape(1, -1),
         positions.reshape(1, -1),
         head_scale,
         gain,
+        skip_rows,
         image,
         w_qkv,
         w_out,

time: 79.5 us -> 78.1 us (0.982)
  Pallas kernels: 76.3 us -> 74.1 us
    pallas_call x1, Pallas kernels: 76.3 us -> 74.1 us  [local(): pl.pallas_call(level_kernel, out_shape=jax.ShapeDtypeStruct(image.shape,...]
where the time goes in v4:
time: 78.1 us; the launch traced here: 76.8 us
  Pallas kernels  74.1 us (95%)
  local copies, waits for them, and re-layouts  2.65 us (3%)
    pallas_call x1, Pallas kernels, local(): pl.pallas_call(level_kernel, out_shape=jax.ShapeDtypeStruct(image.shape,...  74.1 us
    unnamed x1, local copies, waits for them, and re-layouts  2.65 us

profile of v4, /device:TPU:11, one launch (start us, length us, event | category | flops | bytes accessed | tf_op | source)
XLA Modules:
  0.0 76.8 jit_solution(5100048681561800576)
XLA Ops:
  0.0 74.1 %level.1 = bf16[8,128,768]{2,1,0:T(8,128)(2,1)} custom-call(s32[1,1024]{1,0:T(1,128)} %bitcast.2, s32[1,1024]{1,0:T(1,128)} %bitcast.3, f32[12]{0:T(128)} %scale_ref.1, f32[768]{0:T(1024)} %gain_ref.1, bf16[1024,768]{1,0:T(8,128)(2,1)} %rows_ref.1, bf16[8,128,768]{2,1,0:T(8,128)(2,1)} %image_ref.1, bf16[768,2304]{1,0:T(8,128)(2,1)} %w_qkv_ref.1, ...), custom_call_target="tpu_custom_call" | custom-call | tf_op jit(solution)/shard_map/level/pallas_call | solution.py:537
  74.2 2.7 %copy.10 = bf16[8,128,768]{2,1,0:T(8,128)(2,1)} copy(bf16[8,128,768]{2,1,0:T(8,128)(2,1)} %level.1) | data formatting | bytes 3145728

commit v5 on v4

--- a/solution.py
+++ b/solution.py
@@ -84,12 +84,19 @@
                 semaphore, inc=1, device_id=shifted(*peer), device_id_type=MESH
             )
 
-    up_land[...] = jnp.zeros_like(up_land)
-    down_land[...] = jnp.zeros_like(down_land)
     left_land[...] = jnp.zeros_like(left_land)
     right_land[...] = jnp.zeros_like(right_land)
     barrier = pltpu.get_barrier_semaphore()
     signal(barrier, x_peers + y_peers + z_peers)
+
+    @pl.when(my_row == 0)
+    def _():
+        up_land[...] = jnp.zeros_like(up_land)
+
+    @pl.when(my_row == n_row - 1)
+    def _():
+        down_land[...] = jnp.zeros_like(down_land)
+
 
     loads = [
         pltpu.make_async_copy(src, dst, load_sems.at[index])

time: 78.1 us -> 78.1 us (level)
  no operation moved by 1% of the time
where the time goes in v5:
time: 78.1 us; the launch traced here: 76.9 us
  Pallas kernels  74.2 us (95%)
  local copies, waits for them, and re-layouts  2.65 us (3%)
    pallas_call x1, Pallas kernels, local(): pl.pallas_call(level_kernel, out_shape=jax.ShapeDtypeStruct(image.shape,...  74.2 us
    unnamed x1, local copies, waits for them, and re-layouts  2.65 us

profile of v5, /device:TPU:11, one launch (start us, length us, event | category | flops | bytes accessed | tf_op | source)
XLA Modules:
  0.0 76.9 jit_solution(5911579325158069271)
XLA Ops:
  0.0 74.2 %level.1 = bf16[8,128,768]{2,1,0:T(8,128)(2,1)} custom-call(s32[1,1024]{1,0:T(1,128)} %bitcast.2, s32[1,1024]{1,0:T(1,128)} %bitcast.3, f32[12]{0:T(128)} %scale_ref.1, f32[768]{0:T(1024)} %gain_ref.1, bf16[1024,768]{1,0:T(8,128)(2,1)} %rows_ref.1, bf16[8,128,768]{2,1,0:T(8,128)(2,1)} %image_ref.1, bf16[768,2304]{1,0:T(8,128)(2,1)} %w_qkv_ref.1, ...), custom_call_target="tpu_custom_call" | custom-call | tf_op jit(solution)/shard_map/level/pallas_call | solution.py:544
  74.2 2.7 %copy.10 = bf16[8,128,768]{2,1,0:T(8,128)(2,1)} copy(bf16[8,128,768]{2,1,0:T(8,128)(2,1)} %level.1) | data formatting | bytes 3145728
